TPU v7x, 256 devices: a whole 4x4x8 slice. The times are simulated.
256 devices in a mesh: dp: 4 (over y_hi, core), row: 16 (over y_lo, z), col: 4 (over x).
Axes of the slice: x: 4, y: 4 (y_hi: 2, y_lo: 2; y = y_hi * 2 + y_lo), z: 8, core: 2. Of those that a mesh axis runs over, the one named last changes fastest.
Arguments:
- tokens: bfloat16 [1024, 8192], P(('dp', 'row'), 'col'), may hold values from -1.5 to 1.5
- w_gate: bfloat16 [8192, 26624], P(('col', 'dp'), 'row'), may hold values from -0.25 to 0.25
- w_up: bfloat16 [8192, 26624], P(('col', 'dp'), 'row'), may hold values from -0.25 to 0.25
- grad_hidden: bfloat16 [1024, 26624], P(('dp', 'col'), 'row'), may hold values from -6 to 6
Outputs:
- hidden: bfloat16 [1024, 26624], P(('dp', 'col'), 'row')
- grad_tokens: bfloat16 [1024, 8192], P(('dp', 'row'), 'col')
- grad_wgate: float32 [8192, 26624], P(('col', 'dp'), 'row')
- grad_wup: float32 [8192, 26624], P(('col', 'dp'), 'row')
All inputs are finite; a program needn't handle non-finite values.
Results may differ from a plain program's by a relative error of at most 0.011.
Values may be sent and summed in bfloat16 or wider, within the bound.
No kernel may reach another device: no remote copies, remote signals or barrier semaphores. Data moves between devices by JAX's collectives and lax.ppermute only.
A program may use at most 128 MiB of HBM per device.

v0:
```python
import jax
import jax.numpy as jnp
from jax import lax
from jax.experimental import pallas as pl
from jax.experimental.pallas import tpu as pltpu
from jax.sharding import PartitionSpec as P

AXES = ("dp", "row", "col")
MEBI = 1 << 20


def permutation(move):
    pairs = []
    for dp in range(4):
        for row in range(16):
            for col in range(4):
                x, y_hi, y_lo, z, core = move(col, dp // 2, row // 8, row % 8, dp % 2)
                target = ((y_hi * 2 + core) * 16 + y_lo * 8 + z % 8) * 4 + x
                pairs.append(((dp * 16 + row) * 4 + col, target))
    return pairs


def send(array, x=0, y_hi=0, y_lo=0, z=0, core=0):
    return lax.ppermute(
        array,
        AXES,
        permutation(lambda a, b, c, d, e: (a ^ x, b ^ y_hi, c ^ y_lo, d + z, e ^ core)),
    )


def dot(left, right, contract):
    return lax.dot_general(
        left, right, ((contract[:1], contract[1:]), ((), ())), preferred_element_type=jnp.float32
    )


def wide(array):
    return array.astype(jnp.float32)


def narrow(array):
    return array.astype(jnp.bfloat16)


def whole(shape):
    return pl.BlockSpec(shape, lambda i: (0,) * len(shape))


def dot_rows(left, right):
    return dot(left, right, (1, 1))


SMALL = pl.CostEstimate(flops=1 << 20, bytes_accessed=1 << 20, transcendentals=0)


def call(kernel, grid, in_specs, out_specs, out_shape, limit, scratch=()):
    return pl.pallas_call(
        kernel,
        grid=(grid,),
        in_specs=in_specs,
        out_specs=out_specs,
        out_shape=out_shape,
        scratch_shapes=list(scratch),
        compiler_params=pltpu.CompilerParams(vmem_limit_bytes=limit * MEBI),
        cost_estimate=SMALL,
    )


def columns(width):
    return [slice(at, min(width, at + 256)) for at in range(0, width, 256)]


def product(tok, first, second, span):
    feats = first.shape[0]
    return dot(tok[:, :feats], first[:, span], (1, 0)) + dot(tok[:, feats:], second[:, span], (1, 0))


def gate_far_kernel(tok, first, second, out):
    for span in columns(first.shape[1]):
        out[:, span] = narrow(product(tok, first, second, span))


def gate_near_kernel(tok, first, second, far, *outs):
    rows = outs[0].shape[0]
    for span in columns(first.shape[1]):
        total = narrow(product(tok, first, second, span) + wide(far[:, span]))
        for n, out in enumerate(outs):
            out[:, span] = total[n * rows : (n + 1) * rows]


def up_kernel(tok, first, second, *outs):
    rows = outs[0].shape[1]
    for span in columns(first.shape[1]):
        total = narrow(product(tok, first, second, span))
        for n, out in enumerate(outs):
            out[0, :, span] = total[n * rows : (n + 1) * rows]


def gate_far(tok, weights):
    count, feats = tok.shape
    shape = weights[0].shape
    half = pl.BlockSpec((count // 2, feats), lambda i: (1, 0))
    out = (count // 2, shape[1])
    return call(
        gate_far_kernel,
        1,
        [half, whole(shape), whole(shape)],
        whole(out),
        jax.ShapeDtypeStruct(out, jnp.bfloat16),
        24,
    )(tok, *weights)


def gate_near(tok, weights, far):
    count, feats = tok.shape
    shape = weights[0].shape
    half = pl.BlockSpec((count // 2, feats), lambda i: (0, 0))
    out = (count // 8, shape[1])
    return call(
        gate_near_kernel,
        1,
        [half, whole(shape), whole(shape), whole(far.shape)],
        [whole(out)] * 4,
        [jax.ShapeDtypeStruct(out, jnp.bfloat16)] * 4,
        24,
    )(tok, *weights, far)


def up_blocks(tok, weights):
    count, feats = tok.shape
    shape = weights[0].shape
    half = pl.BlockSpec((count // 2, feats), lambda i: (i, 0))
    out = (2, count // 8, shape[1])
    return call(
        up_kernel,
        2,
        [half, whole(shape), whole(shape)],
        [pl.BlockSpec((1,) + out[1:], lambda i: (i, 0, 0))] * 4,
        [jax.ShapeDtypeStruct(out, jnp.bfloat16)] * 4,
        24,
    )(tok, *weights)


def token_grad_kernel(gates, far_gates, ups, undo, wg0, wg1, wu0, wu1, *rest):
    outs, held = rest[:-1], rest[-1]
    rows = gates.shape[0]

    def tile(wg, wu):
        for half, gate in enumerate((gates, far_gates)):
            span = slice(half * rows, (half + 1) * rows)
            held[span, :] = narrow(dot_rows(gate[...], wg[...]) + dot_rows(ups[span, :], wu[...]))

    mine = pl.program_id(0) == 0

    @pl.when(mine)
    def _():
        tile(wg0, wu0)

    @pl.when(jnp.logical_not(mine))
    def _():
        tile(wg1, wu1)

    placed = narrow(dot(undo[...], held[...], (1, 0)))
    size = outs[0].shape[0]
    for n, out in enumerate(outs):
        out[...] = placed[n * size : (n + 1) * size]


def token_grads(gates, far_gates, ups, undo, gate_w, up_w):
    rows, width = gates.shape
    feats = gate_w[0].shape[0]
    out = jax.ShapeDtypeStruct((rows // 2, 2 * feats), jnp.bfloat16)
    return call(
        token_grad_kernel,
        2,
        [whole(gates.shape), whole(gates.shape), whole(ups.shape), whole(undo.shape)]
        + [whole((feats, width))] * 4,
        [pl.BlockSpec((rows // 2, feats), lambda i: (0, i))] * 4,
        [out] * 4,
        36,
        [pltpu.VMEM((2 * rows, feats), jnp.bfloat16)],
    )(gates, far_gates, ups, undo, *gate_w, *up_w)


def weight_grad_kernel(*refs):
    own, other, *grads, out = refs
    rows = grads[0].shape[0]
    for span in columns(out.shape[1]):
        total = None
        for n, grad in enumerate(grads):
            source = own if n < len(grads) // 2 else other
            at = (n % (len(grads) // 2)) * rows
            term = dot(source[:, at : at + rows], grad[:, span], (1, 0))
            total = term if total is None else total + term
        out[:, span] = total


def weight_grad(own, other, grads):
    feats, count = own.shape
    width = grads[0].shape[1]
    side = pl.BlockSpec((feats // 2, count), lambda i: (i, 0))
    return call(
        weight_grad_kernel,
        2,
        [side, side] + [whole(g.shape) for g in grads],
        pl.BlockSpec((feats // 2, width), lambda i: (i, 0)),
        jax.ShapeDtypeStruct((feats, width), jnp.float32),
        24,
    )(own, other, *grads)


def on_device(tokens, w_gate, w_up, grad_hidden):
    feats, width = w_gate.shape
    x = lax.axis_index("col")
    y_hi, core = lax.axis_index("dp") // 2, lax.axis_index("dp") % 2
    y_lo, z = lax.axis_index("row") // 8, lax.axis_index("row") % 8
    rows = tokens.shape[0]
    part = rows
    block = 4 * part

    gate_w = (w_gate, send(w_gate, core=1))
    up_w = (w_up, send(w_up, core=1))

    count = 32 * part
    src = lax.iota(jnp.int32, count)

    def places(d_lo, d_hi, step):
        from_z = (z - step + 8) % 8
        d_x = x ^ ((y_lo ^ d_lo) * 2 + from_z // 4)
        return ((d_hi * 4 + d_x) * 4 + from_z % 4) * part + src % part

    dest = places(src // (16 * part), (src // part) % 2, (src // (2 * part)) % 8)
    order = narrow(lax.broadcasted_iota(jnp.int32, (count, count), 0) == dest[None, :])
    order_turned = narrow(lax.broadcasted_iota(jnp.int32, (count, count), 1) == dest[:, None])
    back = places(src // (16 * part), (src // (8 * part)) % 2, (src // part) % 8)
    undo = narrow(lax.broadcasted_iota(jnp.int32, (count, count), 1) == back[:, None])

    quarters = [
        lax.dynamic_slice_in_dim(tokens, ((y_hi ^ (i // 2)) * 2 + (core ^ (i % 2))) * feats, feats, axis=1)
        for i in range(4)
    ]
    near = jnp.concatenate(quarters[:2], axis=1)
    far = jnp.concatenate(quarters[2:], axis=1)

    def gather_tokens(mine, other):
        piece = jnp.stack([mine, send(other, y_hi=1)])
        piece4 = jnp.stack([send(mine, z=4), send(other, y_hi=1, z=4)])
        pair = jnp.stack([piece, piece4])
        one, seven = send(pair, z=1), send(pair, z=-1)
        two, six = send(piece, z=2), send(piece, z=-2)
        line = jnp.stack([piece, one[0], two, seven[1], piece4, one[1], six, seven[0]])
        flat = jnp.stack([line, send(line, y_lo=1)]).reshape(count, 2 * feats)
        return narrow(dot(order, flat, (1, 0))), narrow(dot(flat, order_turned, (0, 0)))

    def project(tok):
        got = send(gate_far(tok, gate_w), y_hi=1)
        blocks = up_blocks(tok, up_w)
        ups = [send(blocks[k], x=k) for k in (1, 2, 3)]
        up = narrow(sum((wide(u) for u in ups), wide(blocks[0])))
        up_far = send(up[1], y_hi=1)
        gate = gate_near(tok, gate_w, got)
        gates = [send(gate[k], x=k) for k in (1, 2, 3)]
        gate_pre = sum((wide(g) for g in gates), wide(gate[0]))
        return gate_pre, wide(up[0]) + wide(up_far)

    def activate(gate_pre, up_pre, upstream):
        logistic = jax.nn.sigmoid(gate_pre)
        upstream = wide(upstream)
        hidden = narrow(gate_pre * logistic * up_pre)
        grad_up = narrow(upstream * gate_pre * logistic)
        grad_gate = narrow(upstream * up_pre * logistic * (1.0 + gate_pre * (1.0 - logistic)))
        return hidden, grad_gate, grad_up

    def gather_grads(grad_gate, grad_up):
        pair = jnp.stack([grad_up, send(grad_up, y_hi=1)])
        gates = [send(grad_gate, x=k) for k in (2, 1, 3)]
        gates = jnp.concatenate([grad_gate, gates[1], gates[0], gates[2]])
        ups = [send(pair, x=k) for k in (2, 1, 3)]
        far_gates = send(gates, y_hi=1)
        up_all = jnp.stack([pair, ups[1], ups[0], ups[2]], axis=1).reshape(count, width)
        return gates, far_gates, up_all

    def sum_tokens(parts, beside):
        got = [send(parts[1], y_hi=1), send(parts[2], y_lo=1), send(parts[3], y_hi=1, y_lo=1)]
        got, beside = lax.optimization_barrier((got, beside))
        shape = (8, part, 2 * feats)
        line = narrow(
            jnp.stack(
                [
                    (wide(parts[0]) + wide(got[1])).reshape(shape),
                    (wide(got[0]) + wide(got[2])).reshape(shape),
                ],
                axis=1,
            )
        )
        one, seven = send(jnp.stack([line[1], line[5]]), z=-1), send(jnp.stack([line[7], line[3]]), z=1)
        two, six = send(line[2], z=-2), send(line[6], z=2)
        here = wide(line[0]) + wide(one[0]) + wide(seven[0]) + wide(two) + wide(six)
        there = narrow(wide(line[4]) + wide(one[1]) + wide(seven[1]))
        mine, other = narrow(here + wide(send(there, z=4)))
        quarters = [mine[:, :feats], mine[:, feats:], other[:, :feats], other[:, feats:]]
        ordered = []
        for i in range(4):
            a, b = (y_hi == i // 2), (core == i % 2)
            ordered.append(
                jnp.where(
                    a,
                    jnp.where(b, quarters[0], quarters[1]),
                    jnp.where(b, quarters[2], quarters[3]),
                )
            )
        return jnp.concatenate(ordered, axis=1), *beside

    tok, turned = gather_tokens(near, far)
    gate_pre, up_pre = project(tok)
    hidden, grad_gate, grad_up = activate(gate_pre, up_pre, grad_hidden)
    gates, far_gates, ups = gather_grads(grad_gate, grad_up)
    own_turned, other_turned = turned[:feats], send(turned[feats:], core=1)
    gates_too, far_too, ups_too = send(gates, core=1), send(far_gates, core=1), send(ups, core=1)
    parts = token_grads(gates, far_gates, ups, undo, gate_w, up_w)
    grad_wgate = weight_grad(own_turned, other_turned, [gates, far_gates, gates_too, far_too])
    grad_wup = weight_grad(own_turned, other_turned, [ups, ups_too])
    grad_tokens, grad_wgate, grad_wup = sum_tokens(parts, (grad_wgate, grad_wup))
    return (hidden, grad_tokens, grad_wgate, grad_wup)


def solution(mesh):
    placed = (
        P(("dp", "row"), "col"),
        P(("col", "dp"), "row"),
        P(("col", "dp"), "row"),
        P(("dp", "col"), "row"),
    )
    return jax.shard_map(
        on_device,
        mesh=mesh,
        in_specs=placed,
        out_specs=(
            P(("dp", "col"), "row"),
            P(("dp", "row"), "col"),
            P(("col", "dp"), "row"),
            P(("col", "dp"), "row"),
        ),
        check_vma=False,
    )
```

profile of v0, /device:TPU:2, one launch (start us, length us, event | category | flops | bytes accessed | tf_op | source)
XLA Modules:
  0.0 162.8 jit_solution(13606352265935272956)
XLA Ops:
  1.5 9.9 %collective-permute-start.2 = (bf16[16,1024]{1,0:T(8,128)(2,1)S(1)}, bf16[16,1024]{1,0:T(8,128)(2,1)S(1)}, u32[]{:S(2)}, u32[]{:S(2)}) collective-permute-start(bf16[16,1024]{1,0:T(8,128)(2,1)S(1)} %pad_maximum_fusion.11), channel_id=1, source_target_pairs={{0,144},{1,145},{2,146},{3,147},{4,148},{5,149},{6,150},{7,151},{8... | collective-permute-start | bytes 98312 | tf_op jit(solution)/shard_map/ppermute | solution.py:24
  13.3 6.2 %collective-permute-done.1 = bf16[16,1024]{1,0:T(8,128)(2,1)S(1)} collective-permute-done((bf16[16,1024]{1,0:T(8,128)(2,1)S(1)}, bf16[16,1024]{1,0:T(8,128)(2,1)S(1)}, u32[]{:S(2)}, u32[]{:S(2)}) %collective-permute-start.1) | collective-permute-done | bytes 32800 | tf_op jit(solution)/shard_map/ppermute | solution.py:24
  20.9 2.5 %collective-permute-start.5 = (bf16[2,2,16,1024]{3,2,1,0:T(8,128)(2,1)S(1)}, bf16[2,2,16,1024]{3,2,1,0:T(8,128)(2,1)S(1)}, u32[]{:S(2)}, u32[]{:S(2)}) collective-permute-start(bf16[2,2,16,1024]{3,2,1,0:T(8,128)(2,1)S(1)} %pad_maximum_fusion.4), channel_id=1, source_target_pairs={{0,28},{1,29},{2,30},{3,31},{4,0},{5,1},{6,2},{7,3},{8,4},{9,5},{1... | collective-permute-start | bytes 393224 | tf_op jit(solution)/shard_map/ppermute | solution.py:24
  24.2 1.6 %collective-permute-done.3 = bf16[2,2,16,1024]{3,2,1,0:T(8,128)(2,1)S(1)} collective-permute-done((bf16[2,2,16,1024]{3,2,1,0:T(8,128)(2,1)S(1)}, bf16[2,2,16,1024]{3,2,1,0:T(8,128)(2,1)S(1)}, u32[]{:S(2)}, u32[]{:S(2)}) %collective-permute-start.3) | collective-permute-done | bytes 131104 | tf_op jit(solution)/shard_map/ppermute | solution.py:24
  25.8 2.3 %collective-permute-start.6 = (bf16[2,16,1024]{2,1,0:T(8,128)(2,1)S(1)}, bf16[2,16,1024]{2,1,0:T(8,128)(2,1)S(1)}, u32[]{:S(2)}, u32[]{:S(2)}) collective-permute-start(bf16[2,16,1024]{2,1,0:T(8,128)(2,1)S(1)} %get-tuple-element.56), channel_id=1, source_target_pairs={{0,24},{1,25},{2,26},{3,27},{4,28},{5,29},{6,30},{7,31},{8,0},{9,1... | collective-permute-start | bytes 196616 | tf_op jit(solution)/shard_map/ppermute | solution.py:24
  34.6 12.6 %collective-permute-done.7 = bf16[8,2,16,1024]{3,2,1,0:T(8,128)(2,1)} collective-permute-done((bf16[8,2,16,1024]{3,2,1,0:T(8,128)(2,1)}, bf16[8,2,16,1024]{3,2,1,0:T(8,128)(2,1)}, u32[]{:S(2)}, u32[]{:S(2)}) %collective-permute-start.7) | collective-permute-done | bytes 524320 | tf_op jit(solution)/shard_map/ppermute | solution.py:24
  49.9 2.2 %shard_map.77 = (bf16[2,64,1664]{2,1,0:T(8,128)(2,1)S(1)}, bf16[2,64,1664]{2,1,0:T(8,128)(2,1)S(1)}, bf16[2,64,1664]{2,1,0:T(8,128)(2,1)S(1)}, bf16[2,64,1664]{2,1,0:T(8,128)(2,1)S(1)}) custom-call(bf16[512,1024]{1,0:T(8,128)(2,1)S(1)} %convolution_convert_fusion.1.tok, bf16[512,1664]{1,0:T(8,128)(2,1)S(1)} %copy-done.1, ...), custom_call_target="tpu_custom_call" | custom-call | flops 1048576 | bytes 1048576 | tf_op jit(solution)/shard_map/pallas_call | solution.py:134
  52.1 1.6 collective-permute-start.16
  58.3 13.0 %collective-permute-done.16 = bf16[2,64,1664]{2,1,0:T(8,128)(2,1)S(1)} collective-permute-done((bf16[2,64,1664]{2,1,0:T(8,128)(2,1)S(1)}, bf16[2,64,1664]{2,1,0:T(8,128)(2,1)S(1)}, u32[]{:S(2)}, u32[]{:S(2)}) %collective-permute-start.16) | collective-permute-done | bytes 426016 | tf_op jit(solution)/shard_map/ppermute | solution.py:24
  71.3 1.8 %collective-permute-done.14 = bf16[2,64,1664]{2,1,0:T(8,128)(2,1)S(1)} collective-permute-done((bf16[2,64,1664]{2,1,0:T(8,128)(2,1)S(1)}, bf16[2,64,1664]{2,1,0:T(8,128)(2,1)S(1)}, u32[]{:S(2)}, u32[]{:S(2)}) %collective-permute-start.14) | collective-permute-done | bytes 426016 | tf_op jit(solution)/shard_map/ppermute | solution.py:24
  74.7 4.9 %collective-permute-done.9.far = bf16[256,1664]{1,0:T(8,128)(2,1)S(1)} collective-permute-done((bf16[256,1664]{1,0:T(8,128)(2,1)S(1)}, bf16[256,1664]{1,0:T(8,128)(2,1)S(1)}, u32[]{:S(2)}, u32[]{:S(2)}) %collective-permute-start.9) | collective-permute-done | bytes 852000 | tf_op jit(solution)/shard_map/ppermute | solution.py:24
  80.6 1.6 collective-permute-start.12
  82.6 2.2 %collective-permute-start.10 = (bf16[64,1664]{1,0:T(8,128)(2,1)S(1)}, bf16[64,1664]{1,0:T(8,128)(2,1)S(1)}, u32[]{:S(2)}, u32[]{:S(2)}) collective-permute-start(bf16[64,1664]{1,0:T(8,128)(2,1)S(1)} %get-tuple-element.22), channel_id=1, source_target_pairs={{0,1},{1,0},{2,3},{3,2},{4,5},{5,4},{6,7},{7,6},{8,9},{9,8},{10,11... | collective-permute-start | bytes 638984 | tf_op jit(solution)/shard_map/ppermute | solution.py:24
  84.8 1.7 %collective-permute-done.12 = bf16[64,1664]{1,0:T(8,128)(2,1)S(1)} collective-permute-done((bf16[64,1664]{1,0:T(8,128)(2,1)S(1)}, bf16[64,1664]{1,0:T(8,128)(2,1)S(1)}, u32[]{:S(2)}, u32[]{:S(2)}) %collective-permute-start.12) | collective-permute-done | bytes 213024 | tf_op jit(solution)/shard_map/ppermute | solution.py:24
  86.6 3.1 %collective-permute-done.11 = bf16[64,1664]{1,0:T(8,128)(2,1)S(1)} collective-permute-done((bf16[64,1664]{1,0:T(8,128)(2,1)S(1)}, bf16[64,1664]{1,0:T(8,128)(2,1)S(1)}, u32[]{:S(2)}, u32[]{:S(2)}) %collective-permute-start.11) | collective-permute-done | bytes 213024 | tf_op jit(solution)/shard_map/ppermute | solution.py:24
  89.6 1.5 collective-permute-done.10
  94.9 2.1 %collective-permute-start.18 = (bf16[64,1664]{1,0:T(8,128)(2,1)S(1)}, bf16[64,1664]{1,0:T(8,128)(2,1)S(1)}, u32[]{:S(2)}, u32[]{:S(2)}) collective-permute-start(bf16[64,1664]{1,0:T(8,128)(2,1)S(1)} %get-tuple-element.38), channel_id=1, source_target_pairs={{0,1},{1,0},{2,3},{3,2},{4,5},{5,4},{6,7},{7,6},{8,9},{9,8},{10,11... | collective-permute-start | bytes 638984 | tf_op jit(solution)/shard_map/ppermute | solution.py:24
  97.0 2.6 %collective-permute-done.22 = bf16[64,1664]{1,0:T(8,128)(2,1)S(1)} collective-permute-done((bf16[64,1664]{1,0:T(8,128)(2,1)S(1)}, bf16[64,1664]{1,0:T(8,128)(2,1)S(1)}, u32[]{:S(2)}, u32[]{:S(2)}) %collective-permute-start.22) | collective-permute-done | bytes 213024 | tf_op jit(solution)/shard_map/ppermute | solution.py:24
  99.6 2.0 %collective-permute-start.25 = (bf16[2,64,1664]{2,1,0:T(8,128)(2,1)S(1)}, bf16[2,64,1664]{2,1,0:T(8,128)(2,1)S(1)}, u32[]{:S(2)}, u32[]{:S(2)}) collective-permute-start(bf16[2,64,1664]{2,1,0:T(8,128)(2,1)S(1)} %get-tuple-element.50), channel_id=1, source_target_pairs={{0,3},{1,2},{2,1},{3,0},{4,7},{5,6},{6,5},{7,4},{8,11},{9,10},{10,... | collective-permute-start | bytes 1277960 | tf_op jit(solution)/shard_map/ppermute | solution.py:24
  101.7 6.1 %collective-permute-done.20 = bf16[64,1664]{1,0:T(8,128)(2,1)S(1)} collective-permute-done((bf16[64,1664]{1,0:T(8,128)(2,1)S(1)}, bf16[64,1664]{1,0:T(8,128)(2,1)S(1)}, u32[]{:S(2)}, u32[]{:S(2)}) %collective-permute-start.20) | collective-permute-done | bytes 213024 | tf_op jit(solution)/shard_map/ppermute | solution.py:24
  109.3 2.3 %collective-permute-start.21 = (bf16[256,1664]{1,0:T(8,128)(2,1)S(1)}, bf16[256,1664]{1,0:T(8,128)(2,1)S(1)}, u32[]{:S(2)}, u32[]{:S(2)}) collective-permute-start(bf16[256,1664]{1,0:T(8,128)(2,1)S(1)} %pad_maximum_fusion.2.gates.refs_2_), channel_id=1, source_target_pairs={{0,128},{1,129},{2,130},{3,131},{4,132},{5,133},{6,134},{7,135},{8... | collective-permute-start | bytes 2555912 | tf_op jit(solution)/shard_map/ppermute | solution.py:24
  111.5 5.4 %collective-permute-done.25 = bf16[2,64,1664]{2,1,0:T(8,128)(2,1)S(1)} collective-permute-done((bf16[2,64,1664]{2,1,0:T(8,128)(2,1)S(1)}, bf16[2,64,1664]{2,1,0:T(8,128)(2,1)S(1)}, u32[]{:S(2)}, u32[]{:S(2)}) %collective-permute-start.25) | collective-permute-done | bytes 426016 | tf_op jit(solution)/shard_map/ppermute | solution.py:24
  120.3 3.2 %collective-permute-done.21.far_gates.refs_3_ = bf16[256,1664]{1,0:T(8,128)(2,1)S(1)} collective-permute-done((bf16[256,1664]{1,0:T(8,128)(2,1)S(1)}, bf16[256,1664]{1,0:T(8,128)(2,1)S(1)}, u32[]{:S(2)}, u32[]{:S(2)}) %collective-permute-start.21) | collective-permute-done | bytes 852000 | tf_op jit(solution)/shard_map/ppermute | solution.py:24
  124.6 5.2 %shard_map.78 = (bf16[128,1024]{1,0:T(8,128)(2,1)S(1)}, bf16[128,1024]{1,0:T(8,128)(2,1)S(1)}, bf16[128,1024]{1,0:T(8,128)(2,1)S(1)}, bf16[128,1024]{1,0:T(8,128)(2,1)S(1)}) custom-call(bf16[256,1664]{1,0:T(8,128)(2,1)S(1)} %pad_maximum_fusion.2.gates.refs_2_, bf16[256,1664]{1,0:T(8,128)(2,1)S(1)} %collective-permute-done.21.far_gates.refs_3_, ...), custom_call_target="tpu_custom_call" | custom-call | flops 1048576 | bytes 1048576 | tf_op jit(solution)/shard_map/pallas_call | solution.py:173
  129.8 2.3 %collective-permute-start.26 = (bf16[128,1024]{1,0:T(8,128)(2,1)S(1)}, bf16[128,1024]{1,0:T(8,128)(2,1)S(1)}, u32[]{:S(2)}, u32[]{:S(2)}) collective-permute-start(bf16[128,1024]{1,0:T(8,128)(2,1)S(1)} %get-tuple-element.30), channel_id=1, source_target_pairs={{0,128},{1,129},{2,130},{3,131},{4,132},{5,133},{6,134},{7,135},{8... | collective-permute-start | bytes 786440 | tf_op jit(solution)/shard_map/ppermute | solution.py:24
  134.0 3.4 %shard_map.79 = f32[512,1664]{1,0:T(8,128)} custom-call(bf16[512,512]{1,0:T(8,128)(2,1)S(1)} %get-tuple-element.42.refs_0_, bf16[512,512]{1,0:T(8,128)(2,1)S(1)} %collective-permute-done.29.refs_1_, bf16[256,1664]{1,0:T(8,128)(2,1)S(1)} %pad_maximum_fusion.2.gates.refs_2_, bf16[256,1664]{1,0:T(8,128)(2,1)S(1)} %collective-permute-done.21.far_gates.refs_3_, ...), custom_call_target="tpu_custom_call" | custom-call | flops 1048576 | bytes 1048576 | tf_op jit(solution)/shard_map/pallas_call | solution.py:202
  137.4 3.4 %shard_map.80 = f32[512,1664]{1,0:T(8,128)} custom-call(bf16[512,512]{1,0:T(8,128)(2,1)S(1)} %get-tuple-element.42.refs_0_, bf16[512,512]{1,0:T(8,128)(2,1)S(1)} %collective-permute-done.29.refs_1_, bf16[512,1664]{1,0:T(8,128)(2,1)S(1)} %bitcast.64, bf16[512,1664]{1,0:T(8,128)(2,1)S(1)} %collective-permute-done.32.refs_3_), custom_call_target="tpu_custom_call" | custom-call | flops 1048576 | bytes 1048576 | tf_op jit(solution)/shard_map/pallas_call | solution.py:202
  140.8 3.6 %collective-permute-done.27 = bf16[128,1024]{1,0:T(8,128)(2,1)S(1)} collective-permute-done((bf16[128,1024]{1,0:T(8,128)(2,1)S(1)}, bf16[128,1024]{1,0:T(8,128)(2,1)S(1)}, u32[]{:S(2)}, u32[]{:S(2)}) %collective-permute-start.27) | collective-permute-done | bytes 262176 | tf_op jit(solution)/shard_map/ppermute | solution.py:24
  145.6 3.3 %collective-permute-start.33 = (bf16[2,2,16,1024]{3,2,1,0:T(8,128)(2,1)S(1)}, bf16[2,2,16,1024]{3,2,1,0:T(8,128)(2,1)S(1)}, u32[]{:S(2)}, u32[]{:S(2)}) collective-permute-start(bf16[2,2,16,1024]{3,2,1,0:T(8,128)(2,1)S(1)} %pad_maximum_fusion.5), channel_id=1, source_target_pairs={{0,28},{1,29},{2,30},{3,31},{4,0},{5,1},{6,2},{7,3},{8,4},{9,5},{1... | collective-permute-start | bytes 393224 | tf_op jit(solution)/shard_map/ppermute | solution.py:24
  149.2 3.8 %collective-permute-start.35 = (bf16[2,16,1024]{2,1,0:T(8,128)(2,1)S(1)}, bf16[2,16,1024]{2,1,0:T(8,128)(2,1)S(1)}, u32[]{:S(2)}, u32[]{:S(2)}) collective-permute-start(bf16[2,16,1024]{2,1,0:T(8,128)(2,1)S(1)} %get-tuple-element.43), channel_id=1, source_target_pairs={{0,24},{1,25},{2,26},{3,27},{4,28},{5,29},{6,30},{7,31},{8,0},{9,1... | collective-permute-start | bytes 196616 | tf_op jit(solution)/shard_map/ppermute | solution.py:24
  153.1 4.0 %collective-permute-start.37 = (bf16[2,16,1024]{2,1,0:T(8,128)(2,1)S(1)}, bf16[2,16,1024]{2,1,0:T(8,128)(2,1)S(1)}, u32[]{:S(2)}, u32[]{:S(2)}) collective-permute-start(bf16[2,16,1024]{2,1,0:T(8,128)(2,1)S(1)} %fusion.18), channel_id=1, source_target_pairs={{0,16},{1,17},{2,18},{3,19},{4,20},{5,21},{6,22},{7,23},{8,24},{9,... | collective-permute-start | bytes 196616 | tf_op jit(solution)/shard_map/ppermute | solution.py:24
  157.1 5.0 %collective-permute-done.37 = bf16[2,16,1024]{2,1,0:T(8,128)(2,1)S(1)} collective-permute-done((bf16[2,16,1024]{2,1,0:T(8,128)(2,1)S(1)}, bf16[2,16,1024]{2,1,0:T(8,128)(2,1)S(1)}, u32[]{:S(2)}, u32[]{:S(2)}) %collective-permute-start.37) | collective-permute-done | bytes 65568 | tf_op jit(solution)/shard_map/ppermute | solution.py:24
  (94 shorter events, 35.4 us)
Async XLA Ops:
  1.5 11.8 %collective-permute-start.2 = (bf16[16,1024]{1,0:T(8,128)(2,1)S(1)}, bf16[16,1024]{1,0:T(8,128)(2,1)S(1)}, u32[]{:S(2)}, u32[]{:S(2)}) collective-permute-start(bf16[16,1024]{1,0:T(8,128)(2,1)S(1)} %pad_maximum_fusion.11), channel_id=1, source_target_pairs={{0,144},{1,145},{2,146},{3,147},{4,148},{5,149},{6,150},{7,151},{8... | collective-permute-start | bytes 98312 | tf_op jit(solution)/shard_map/ppermute | solution.py:24
  11.4 8.1 %collective-permute-start.1 = (bf16[16,1024]{1,0:T(8,128)(2,1)S(1)}, bf16[16,1024]{1,0:T(8,128)(2,1)S(1)}, u32[]{:S(2)}, u32[]{:S(2)}) collective-permute-start(bf16[16,1024]{1,0:T(8,128)(2,1)S(1)} %get-tuple-element.62), channel_id=1, source_target_pairs={{0,16},{1,17},{2,18},{3,19},{4,20},{5,21},{6,22},{7,23},{8,24},{9,... | collective-permute-start | bytes 98312 | tf_op jit(solution)/shard_map/ppermute | solution.py:24
  11.4 8.1 %collective-permute-start = (bf16[16,1024]{1,0:T(8,128)(2,1)S(1)}, bf16[16,1024]{1,0:T(8,128)(2,1)S(1)}, u32[]{:S(2)}, u32[]{:S(2)}) collective-permute-start(bf16[16,1024]{1,0:T(8,128)(2,1)S(1)} %pad_maximum_fusion.11), channel_id=1, source_target_pairs={{0,128},{1,129},{2,130},{3,131},{4,132},{5,133},{6,134},{7,135},{8... | collective-permute-start | bytes 98312 | tf_op jit(solution)/shard_map/ppermute | solution.py:24
  20.4 28.8 %collective-permute-start.13 = (bf16[512,1664]{1,0:T(8,128)(2,1)}, bf16[512,1664]{1,0:T(8,128)(2,1)S(1)}, u32[]{:S(2)}, u32[]{:S(2)}) collective-permute-start(bf16[512,1664]{1,0:T(8,128)(2,1)} %wu0.1), channel_id=1, source_target_pairs={{0,64},{1,65},{2,66},{3,67},{4,68},{5,69},{6,70},{7,71},{8,72},{9,... | collective-permute-start | bytes 5111816 | tf_op jit(solution)/shard_map/ppermute | solution.py:24
  20.4 35.9 %collective-permute-start.8 = (bf16[512,1664]{1,0:T(8,128)(2,1)}, bf16[512,1664]{1,0:T(8,128)(2,1)S(1)}, u32[]{:S(2)}, u32[]{:S(2)}) collective-permute-start(bf16[512,1664]{1,0:T(8,128)(2,1)} %wg0.1), channel_id=1, source_target_pairs={{0,64},{1,65},{2,66},{3,67},{4,68},{5,69},{6,70},{7,71},{8,72},{9,... | collective-permute-start | bytes 5111816 | tf_op jit(solution)/shard_map/ppermute | solution.py:24
  20.9 9.8 %collective-permute-start.5 = (bf16[2,2,16,1024]{3,2,1,0:T(8,128)(2,1)S(1)}, bf16[2,2,16,1024]{3,2,1,0:T(8,128)(2,1)S(1)}, u32[]{:S(2)}, u32[]{:S(2)}) collective-permute-start(bf16[2,2,16,1024]{3,2,1,0:T(8,128)(2,1)S(1)} %pad_maximum_fusion.4), channel_id=1, source_target_pairs={{0,28},{1,29},{2,30},{3,31},{4,0},{5,1},{6,2},{7,3},{8,4},{9,5},{1... | collective-permute-start | bytes 393224 | tf_op jit(solution)/shard_map/ppermute | solution.py:24
  33.9 13.3 %collective-permute-start.7 = (bf16[8,2,16,1024]{3,2,1,0:T(8,128)(2,1)}, bf16[8,2,16,1024]{3,2,1,0:T(8,128)(2,1)}, u32[]{:S(2)}, u32[]{:S(2)}) collective-permute-start(bf16[8,2,16,1024]{3,2,1,0:T(8,128)(2,1)} %slice_dynamic-update-slice_fusion), channel_id=1, source_target_pairs={{0,32},{1,33},{2,34},{3,35},{4,36},{5,37},{6,38},{7,39},{8,40},{9,... | collective-permute-start | bytes 1572872 | tf_op jit(solution)/shard_map/ppermute | solution.py:24
  52.1 19.1 %collective-permute-start.16 = (bf16[2,64,1664]{2,1,0:T(8,128)(2,1)S(1)}, bf16[2,64,1664]{2,1,0:T(8,128)(2,1)S(1)}, u32[]{:S(2)}, u32[]{:S(2)}) collective-permute-start(bf16[2,64,1664]{2,1,0:T(8,128)(2,1)S(1)} %get-tuple-element.28), channel_id=1, source_target_pairs={{0,3},{1,2},{2,1},{3,0},{4,7},{5,6},{6,5},{7,4},{8,11},{9,10},{10,... | collective-permute-start | bytes 1277960 | tf_op jit(solution)/shard_map/ppermute | solution.py:24
  53.7 17.6 %collective-permute-start.15 = (bf16[2,64,1664]{2,1,0:T(8,128)(2,1)S(1)}, bf16[2,64,1664]{2,1,0:T(8,128)(2,1)S(1)}, u32[]{:S(2)}, u32[]{:S(2)}) collective-permute-start(bf16[2,64,1664]{2,1,0:T(8,128)(2,1)S(1)} %get-tuple-element.27), channel_id=1, source_target_pairs={{0,2},{1,3},{2,0},{3,1},{4,6},{5,7},{6,4},{7,5},{8,10},{9,11},{10,... | collective-permute-start | bytes 1277960 | tf_op jit(solution)/shard_map/ppermute | solution.py:24
  54.8 18.3 %collective-permute-start.14 = (bf16[2,64,1664]{2,1,0:T(8,128)(2,1)S(1)}, bf16[2,64,1664]{2,1,0:T(8,128)(2,1)S(1)}, u32[]{:S(2)}, u32[]{:S(2)}) collective-permute-start(bf16[2,64,1664]{2,1,0:T(8,128)(2,1)S(1)} %get-tuple-element.26), channel_id=1, source_target_pairs={{0,1},{1,0},{2,3},{3,2},{4,5},{5,4},{6,7},{7,6},{8,9},{9,8},{10,11... | collective-permute-start | bytes 1277960 | tf_op jit(solution)/shard_map/ppermute | solution.py:24
  57.4 22.1 %collective-permute-start.9 = (bf16[256,1664]{1,0:T(8,128)(2,1)S(1)}, bf16[256,1664]{1,0:T(8,128)(2,1)S(1)}, u32[]{:S(2)}, u32[]{:S(2)}) collective-permute-start(bf16[256,1664]{1,0:T(8,128)(2,1)S(1)} %shard_map.75), channel_id=1, source_target_pairs={{0,128},{1,129},{2,130},{3,131},{4,132},{5,133},{6,134},{7,135},{8... | collective-permute-start | bytes 2555912 | tf_op jit(solution)/shard_map/ppermute | solution.py:24
  73.3 11.5 %collective-permute-start.17 = (bf16[64,1664]{1,0:T(8,128)(2,1)S(1)}, bf16[64,1664]{1,0:T(8,128)(2,1)S(1)}, u32[]{:S(2)}, u32[]{:S(2)}) collective-permute-start(bf16[64,1664]{1,0:T(8,128)(2,1)S(1)} %slice_bitcast_fusion), channel_id=1, source_target_pairs={{0,128},{1,129},{2,130},{3,131},{4,132},{5,133},{6,134},{7,135},{8... | collective-permute-start | bytes 638984 | tf_op jit(solution)/shard_map/ppermute | solution.py:24
  82.6 8.6 %collective-permute-start.10 = (bf16[64,1664]{1,0:T(8,128)(2,1)S(1)}, bf16[64,1664]{1,0:T(8,128)(2,1)S(1)}, u32[]{:S(2)}, u32[]{:S(2)}) collective-permute-start(bf16[64,1664]{1,0:T(8,128)(2,1)S(1)} %get-tuple-element.22), channel_id=1, source_target_pairs={{0,1},{1,0},{2,3},{3,2},{4,5},{5,4},{6,7},{7,6},{8,9},{9,8},{10,11... | collective-permute-start | bytes 638984 | tf_op jit(solution)/shard_map/ppermute | solution.py:24
  92.9 14.9 %collective-permute-start.20 = (bf16[64,1664]{1,0:T(8,128)(2,1)S(1)}, bf16[64,1664]{1,0:T(8,128)(2,1)S(1)}, u32[]{:S(2)}, u32[]{:S(2)}) collective-permute-start(bf16[64,1664]{1,0:T(8,128)(2,1)S(1)} %get-tuple-element.38), channel_id=1, source_target_pairs={{0,3},{1,2},{2,1},{3,0},{4,7},{5,6},{6,5},{7,4},{8,11},{9,10},{10,... | collective-permute-start | bytes 638984 | tf_op jit(solution)/shard_map/ppermute | solution.py:24
  94.4 14.8 %collective-permute-start.19 = (bf16[64,1664]{1,0:T(8,128)(2,1)S(1)}, bf16[64,1664]{1,0:T(8,128)(2,1)S(1)}, u32[]{:S(2)}, u32[]{:S(2)}) collective-permute-start(bf16[64,1664]{1,0:T(8,128)(2,1)S(1)} %get-tuple-element.38), channel_id=1, source_target_pairs={{0,2},{1,3},{2,0},{3,1},{4,6},{5,7},{6,4},{7,5},{8,10},{9,11},{10,... | collective-permute-start | bytes 638984 | tf_op jit(solution)/shard_map/ppermute | solution.py:24
  94.9 14.3 %collective-permute-start.18 = (bf16[64,1664]{1,0:T(8,128)(2,1)S(1)}, bf16[64,1664]{1,0:T(8,128)(2,1)S(1)}, u32[]{:S(2)}, u32[]{:S(2)}) collective-permute-start(bf16[64,1664]{1,0:T(8,128)(2,1)S(1)} %get-tuple-element.38), channel_id=1, source_target_pairs={{0,1},{1,0},{2,3},{3,2},{4,5},{5,4},{6,7},{7,6},{8,9},{9,8},{10,11... | collective-permute-start | bytes 638984 | tf_op jit(solution)/shard_map/ppermute | solution.py:24
  99.6 17.3 %collective-permute-start.25 = (bf16[2,64,1664]{2,1,0:T(8,128)(2,1)S(1)}, bf16[2,64,1664]{2,1,0:T(8,128)(2,1)S(1)}, u32[]{:S(2)}, u32[]{:S(2)}) collective-permute-start(bf16[2,64,1664]{2,1,0:T(8,128)(2,1)S(1)} %get-tuple-element.50), channel_id=1, source_target_pairs={{0,3},{1,2},{2,1},{3,0},{4,7},{5,6},{6,5},{7,4},{8,11},{9,10},{10,... | collective-permute-start | bytes 1277960 | tf_op jit(solution)/shard_map/ppermute | solution.py:24
  101.7 15.3 %collective-permute-start.24 = (bf16[2,64,1664]{2,1,0:T(8,128)(2,1)S(1)}, bf16[2,64,1664]{2,1,0:T(8,128)(2,1)S(1)}, u32[]{:S(2)}, u32[]{:S(2)}) collective-permute-start(bf16[2,64,1664]{2,1,0:T(8,128)(2,1)S(1)} %get-tuple-element.50), channel_id=1, source_target_pairs={{0,2},{1,3},{2,0},{3,1},{4,6},{5,7},{6,4},{7,5},{8,10},{9,11},{10,... | collective-permute-start | bytes 1277960 | tf_op jit(solution)/shard_map/ppermute | solution.py:24
  107.8 10.7 %collective-permute-start.23 = (bf16[2,64,1664]{2,1,0:T(8,128)(2,1)S(1)}, bf16[2,64,1664]{2,1,0:T(8,128)(2,1)S(1)}, u32[]{:S(2)}, u32[]{:S(2)}) collective-permute-start(bf16[2,64,1664]{2,1,0:T(8,128)(2,1)S(1)} %get-tuple-element.50), channel_id=1, source_target_pairs={{0,1},{1,0},{2,3},{3,2},{4,5},{5,4},{6,7},{7,6},{8,9},{9,8},{10,11... | collective-permute-start | bytes 1277960 | tf_op jit(solution)/shard_map/ppermute | solution.py:24
  109.3 14.3 %collective-permute-start.21 = (bf16[256,1664]{1,0:T(8,128)(2,1)S(1)}, bf16[256,1664]{1,0:T(8,128)(2,1)S(1)}, u32[]{:S(2)}, u32[]{:S(2)}) collective-permute-start(bf16[256,1664]{1,0:T(8,128)(2,1)S(1)} %pad_maximum_fusion.2.gates.refs_2_), channel_id=1, source_target_pairs={{0,128},{1,129},{2,130},{3,131},{4,132},{5,133},{6,134},{7,135},{8... | collective-permute-start | bytes 2555912 | tf_op jit(solution)/shard_map/ppermute | solution.py:24
  118.9 18.5 %collective-permute-start.32 = (bf16[512,1664]{1,0:T(8,128)(2,1)S(1)}, bf16[512,1664]{1,0:T(8,128)(2,1)S(1)}, u32[]{:S(2)}, u32[]{:S(2)}) collective-permute-start(bf16[512,1664]{1,0:T(8,128)(2,1)S(1)} %bitcast.62), channel_id=1, source_target_pairs={{0,64},{1,65},{2,66},{3,67},{4,68},{5,69},{6,70},{7,71},{8,72},{9,... | collective-permute-start | bytes 5111816 | tf_op jit(solution)/shard_map/ppermute | solution.py:24
  119.0 13.6 %collective-permute-start.30 = (bf16[256,1664]{1,0:T(8,128)(2,1)S(1)}, bf16[256,1664]{1,0:T(8,128)(2,1)S(1)}, u32[]{:S(2)}, u32[]{:S(2)}) collective-permute-start(bf16[256,1664]{1,0:T(8,128)(2,1)S(1)} %pad_maximum_fusion.2.gates.refs_2_), channel_id=1, source_target_pairs={{0,64},{1,65},{2,66},{3,67},{4,68},{5,69},{6,70},{7,71},{8,72},{9,... | collective-permute-start | bytes 2555912 | tf_op jit(solution)/shard_map/ppermute | solution.py:24
  123.5 10.4 %collective-permute-start.31 = (bf16[256,1664]{1,0:T(8,128)(2,1)S(1)}, bf16[256,1664]{1,0:T(8,128)(2,1)S(1)}, u32[]{:S(2)}, u32[]{:S(2)}) collective-permute-start(bf16[256,1664]{1,0:T(8,128)(2,1)S(1)} %collective-permute-done.21.far_gates.refs_3_), channel_id=1, source_target_pairs={{0,64},{1,65},{2,66},{3,67},{4,68},{5,69},{6,70},{7,71},{8,72},{9,... | collective-permute-start | bytes 2555912 | tf_op jit(solution)/shard_map/ppermute | solution.py:24
  123.6 8.4 %collective-permute-start.29 = (bf16[512,512]{1,0:T(8,128)(2,1)S(1)}, bf16[512,512]{1,0:T(8,128)(2,1)S(1)}, u32[]{:S(2)}, u32[]{:S(2)}) collective-permute-start(bf16[512,512]{1,0:T(8,128)(2,1)S(1)} %get-tuple-element.41), channel_id=1, source_target_pairs={{0,64},{1,65},{2,66},{3,67},{4,68},{5,69},{6,70},{7,71},{8,72},{9,... | collective-permute-start | bytes 1572872 | tf_op jit(solution)/shard_map/ppermute | solution.py:24
  129.8 11.1 %collective-permute-start.26 = (bf16[128,1024]{1,0:T(8,128)(2,1)S(1)}, bf16[128,1024]{1,0:T(8,128)(2,1)S(1)}, u32[]{:S(2)}, u32[]{:S(2)}) collective-permute-start(bf16[128,1024]{1,0:T(8,128)(2,1)S(1)} %get-tuple-element.30), channel_id=1, source_target_pairs={{0,128},{1,129},{2,130},{3,131},{4,132},{5,133},{6,134},{7,135},{8... | collective-permute-start | bytes 786440 | tf_op jit(solution)/shard_map/ppermute | solution.py:24
  132.1 12.4 %collective-permute-start.27 = (bf16[128,1024]{1,0:T(8,128)(2,1)S(1)}, bf16[128,1024]{1,0:T(8,128)(2,1)S(1)}, u32[]{:S(2)}, u32[]{:S(2)}) collective-permute-start(bf16[128,1024]{1,0:T(8,128)(2,1)S(1)} %get-tuple-element.31), channel_id=1, source_target_pairs={{0,32},{1,33},{2,34},{3,35},{4,36},{5,37},{6,38},{7,39},{8,40},{9,... | collective-permute-start | bytes 786440 | tf_op jit(solution)/shard_map/ppermute | solution.py:24
  132.6 12.6 %collective-permute-start.28 = (bf16[128,1024]{1,0:T(8,128)(2,1)S(1)}, bf16[128,1024]{1,0:T(8,128)(2,1)S(1)}, u32[]{:S(2)}, u32[]{:S(2)}) collective-permute-start(bf16[128,1024]{1,0:T(8,128)(2,1)S(1)} %get-tuple-element.32), channel_id=1, source_target_pairs={{0,160},{1,161},{2,162},{3,163},{4,164},{5,165},{6,166},{7,167},{8... | collective-permute-start | bytes 786440 | tf_op jit(solution)/shard_map/ppermute | solution.py:24
  145.5 7.5 %collective-permute-start.34 = (bf16[2,2,16,1024]{3,2,1,0:T(8,128)(2,1)S(1)}, bf16[2,2,16,1024]{3,2,1,0:T(8,128)(2,1)S(1)}, u32[]{:S(2)}, u32[]{:S(2)}) collective-permute-start(bf16[2,2,16,1024]{3,2,1,0:T(8,128)(2,1)S(1)} %pad_maximum_fusion.6), channel_id=1, source_target_pairs={{0,4},{1,5},{2,6},{3,7},{4,8},{5,9},{6,10},{7,11},{8,12},{9,13},{1... | collective-permute-start | bytes 393224 | tf_op jit(solution)/shard_map/ppermute | solution.py:24
  145.6 7.4 %collective-permute-start.33 = (bf16[2,2,16,1024]{3,2,1,0:T(8,128)(2,1)S(1)}, bf16[2,2,16,1024]{3,2,1,0:T(8,128)(2,1)S(1)}, u32[]{:S(2)}, u32[]{:S(2)}) collective-permute-start(bf16[2,2,16,1024]{3,2,1,0:T(8,128)(2,1)S(1)} %pad_maximum_fusion.5), channel_id=1, source_target_pairs={{0,28},{1,29},{2,30},{3,31},{4,0},{5,1},{6,2},{7,3},{8,4},{9,5},{1... | collective-permute-start | bytes 393224 | tf_op jit(solution)/shard_map/ppermute | solution.py:24
  148.9 8.2 %collective-permute-start.36 = (bf16[2,16,1024]{2,1,0:T(8,128)(2,1)S(1)}, bf16[2,16,1024]{2,1,0:T(8,128)(2,1)S(1)}, u32[]{:S(2)}, u32[]{:S(2)}) collective-permute-start(bf16[2,16,1024]{2,1,0:T(8,128)(2,1)S(1)} %get-tuple-element.48), channel_id=1, source_target_pairs={{0,8},{1,9},{2,10},{3,11},{4,12},{5,13},{6,14},{7,15},{8,16},{9,17... | collective-permute-start | bytes 196616 | tf_op jit(solution)/shard_map/ppermute | solution.py:24
  149.2 7.8 %collective-permute-start.35 = (bf16[2,16,1024]{2,1,0:T(8,128)(2,1)S(1)}, bf16[2,16,1024]{2,1,0:T(8,128)(2,1)S(1)}, u32[]{:S(2)}, u32[]{:S(2)}) collective-permute-start(bf16[2,16,1024]{2,1,0:T(8,128)(2,1)S(1)} %get-tuple-element.43), channel_id=1, source_target_pairs={{0,24},{1,25},{2,26},{3,27},{4,28},{5,29},{6,30},{7,31},{8,0},{9,1... | collective-permute-start | bytes 196616 | tf_op jit(solution)/shard_map/ppermute | solution.py:24
  153.1 9.0 %collective-permute-start.37 = (bf16[2,16,1024]{2,1,0:T(8,128)(2,1)S(1)}, bf16[2,16,1024]{2,1,0:T(8,128)(2,1)S(1)}, u32[]{:S(2)}, u32[]{:S(2)}) collective-permute-start(bf16[2,16,1024]{2,1,0:T(8,128)(2,1)S(1)} %fusion.18), channel_id=1, source_target_pairs={{0,16},{1,17},{2,18},{3,19},{4,20},{5,21},{6,22},{7,23},{8,24},{9,... | collective-permute-start | bytes 196616 | tf_op jit(solution)/shard_map/ppermute | solution.py:24
  (9 other events, 66.9 us)
where the time goes:
time: 163 us
  waiting for transfers between devices  77.1 us (47%)
  starting transfers between devices  55.6 us (34%)
  Pallas kernels  16.5 us (10%)
  local copies, waits for them, and re-layouts  5.53 us (3%)
  other arithmetic  5.47 us (3%)
    ppermute x38, waiting for transfers between devices, send(): lax.ppermute(array, AXES, permutation(lambda a, b, c, d, e: (a ^ x, b ^ y...  77.1 us
    ppermute x38, starting transfers between devices, send(): lax.ppermute(array, AXES, permutation(lambda a, b, c, d, e: (a ^ x, b ^ y...  55.6 us
    pallas_call x2, Pallas kernels, weight_grad(): call(weight_grad_kernel, 2, [side, side] + [whole(g.shape) for g in grads...  6.85 us
    pallas_call x1, Pallas kernels, token_grads(): call(token_grad_kernel, 2, [whole(gates.shape), whole(gates.shape), whole...  5.16 us
    unnamed x11, local copies, waits for them, and re-layouts  3.89 us
  transfers between devices with their start and end apart: 38, of which 19 were waited for; matrix products, arithmetic and copies ran while one was open for 6% of the time, Pallas kernels for 10%

commit v1 on v0

--- a/solution.py
+++ b/solution.py
@@ -1,3 +1,5 @@
+import functools
+
 import jax
 import jax.numpy as jnp
 from jax import lax
@@ -43,7 +45,7 @@
 
 
 def whole(shape):
-    return pl.BlockSpec(shape, lambda i: (0,) * len(shape))
+    return pl.BlockSpec(memory_space=pltpu.VMEM)
 
 
 def dot_rows(left, right):
@@ -70,75 +72,119 @@
     return [slice(at, min(width, at + 256)) for at in range(0, width, 256)]
 
 
-def product(tok, first, second, span):
-    feats = first.shape[0]
-    return dot(tok[:, :feats], first[:, span], (1, 0)) + dot(tok[:, feats:], second[:, span], (1, 0))
-
-
-def gate_far_kernel(tok, first, second, out):
+def product(near, far, first, second, span):
+    return dot(near[...], first[:, span], (1, 0)) + dot(far[...], second[:, span], (1, 0))
+
+
+def gate_far_kernel(near, distant, first, second, out):
     for span in columns(first.shape[1]):
-        out[:, span] = narrow(product(tok, first, second, span))
-
-
-def gate_near_kernel(tok, first, second, far, *outs):
+        out[:, span] = narrow(product(near, distant, first, second, span))
+
+
+def gate_near_kernel(near, distant, first, second, far, *outs):
     rows = outs[0].shape[0]
     for span in columns(first.shape[1]):
-        total = narrow(product(tok, first, second, span) + wide(far[:, span]))
+        total = narrow(product(near, distant, first, second, span) + wide(far[:, span]))
         for n, out in enumerate(outs):
             out[:, span] = total[n * rows : (n + 1) * rows]
 
 
-def up_kernel(tok, first, second, *outs):
+def up_kernel(near, distant, first, second, *outs):
     rows = outs[0].shape[1]
     for span in columns(first.shape[1]):
-        total = narrow(product(tok, first, second, span))
+        total = narrow(product(near, distant, first, second, span))
         for n, out in enumerate(outs):
             out[0, :, span] = total[n * rows : (n + 1) * rows]
 
 
 def gate_far(tok, weights):
-    count, feats = tok.shape
+    count, feats = tok[0].shape
     shape = weights[0].shape
     half = pl.BlockSpec((count // 2, feats), lambda i: (1, 0))
     out = (count // 2, shape[1])
     return call(
         gate_far_kernel,
         1,
-        [half, whole(shape), whole(shape)],
+        [half, half, whole(shape), whole(shape)],
         whole(out),
         jax.ShapeDtypeStruct(out, jnp.bfloat16),
-        24,
-    )(tok, *weights)
+        12,
+    )(*tok, *weights)
 
 
 def gate_near(tok, weights, far):
-    count, feats = tok.shape
+    count, feats = tok[0].shape
     shape = weights[0].shape
     half = pl.BlockSpec((count // 2, feats), lambda i: (0, 0))
     out = (count // 8, shape[1])
     return call(
         gate_near_kernel,
         1,
-        [half, whole(shape), whole(shape), whole(far.shape)],
+        [half, half, whole(shape), whole(shape), whole(far.shape)],
         [whole(out)] * 4,
         [jax.ShapeDtypeStruct(out, jnp.bfloat16)] * 4,
-        24,
-    )(tok, *weights, far)
+        12,
+    )(*tok, *weights, far)
 
 
 def up_blocks(tok, weights):
-    count, feats = tok.shape
+    count, feats = tok[0].shape
     shape = weights[0].shape
     half = pl.BlockSpec((count // 2, feats), lambda i: (i, 0))
     out = (2, count // 8, shape[1])
     return call(
         up_kernel,
         2,
-        [half, whole(shape), whole(shape)],
+        [half, half, whole(shape), whole(shape)],
         [pl.BlockSpec((1,) + out[1:], lambda i: (i, 0, 0))] * 4,
         [jax.ShapeDtypeStruct(out, jnp.bfloat16)] * 4,
-        24,
-    )(tok, *weights)
+        12,
+    )(*tok, *weights)
+
+
+def join_kernel(count, *refs):
+    arrays, outs = refs[:count], refs[count:]
+    for out in outs:
+        at = 0
+        for array in arrays:
+            rows = array.shape[0]
+            if at + rows <= out.shape[0]:
+                out[at : at + rows, :] = array[...]
+            at += rows
+
+
+def join(arrays, lengths):
+    width = arrays[0].shape[1]
+    return call(
+        functools.partial(join_kernel, len(arrays)),
+        1,
+        [whole(a.shape) for a in arrays],
+        [whole((n, width)) for n in lengths],
+        [jax.ShapeDtypeStruct((n, width), jnp.bfloat16) for n in lengths],
+        8,
+    )(*arrays)
+
+
+def place_kernel(first, second, order, *outs):
+    half, feats = first.shape[0], first.shape[1] // 2
+    for n, out in enumerate(outs):
+        span = slice(n * feats, (n + 1) * feats)
+        out[...] = narrow(
+            dot(order[:, :half], first[:, span], (1, 0))
+            + dot(order[:, half:], second[:, span], (1, 0))
+        )
+
+
+def place(first, second, order):
+    out = (order.shape[0], first.shape[1] // 2)
+    return call(
+        place_kernel,
+        1,
+        [whole(first.shape), whole(second.shape), whole(order.shape)],
+        [whole(out)] * 2,
+        [jax.ShapeDtypeStruct(out, jnp.bfloat16)] * 2,
+        12,
+    )(first, second, order)
 
 
 def token_grad_kernel(gates, far_gates, ups, undo, wg0, wg1, wu0, wu1, *rest):
@@ -177,7 +223,7 @@
         + [whole((feats, width))] * 4,
         [pl.BlockSpec((rows // 2, feats), lambda i: (0, i))] * 4,
         [out] * 4,
-        36,
+        16,
         [pltpu.VMEM((2 * rows, feats), jnp.bfloat16)],
     )(gates, far_gates, ups, undo, *gate_w, *up_w)
 
@@ -190,22 +236,22 @@
         for n, grad in enumerate(grads):
             source = own if n < len(grads) // 2 else other
             at = (n % (len(grads) // 2)) * rows
-            term = dot(source[:, at : at + rows], grad[:, span], (1, 0))
+            term = dot(source[at : at + rows, :], grad[:, span], (0, 0))
             total = term if total is None else total + term
         out[:, span] = total
 
 
 def weight_grad(own, other, grads):
-    feats, count = own.shape
+    count, feats = own.shape
     width = grads[0].shape[1]
-    side = pl.BlockSpec((feats // 2, count), lambda i: (i, 0))
+    side = pl.BlockSpec((count, feats // 2), lambda i: (0, i))
     return call(
         weight_grad_kernel,
         2,
         [side, side] + [whole(g.shape) for g in grads],
         pl.BlockSpec((feats // 2, width), lambda i: (i, 0)),
         jax.ShapeDtypeStruct((feats, width), jnp.float32),
-        24,
+        12,
     )(own, other, *grads)
 
 
@@ -218,6 +264,7 @@
     part = rows
     block = 4 * part
 
+
     gate_w = (w_gate, send(w_gate, core=1))
     up_w = (w_up, send(w_up, core=1))
 
@@ -229,9 +276,10 @@
         d_x = x ^ ((y_lo ^ d_lo) * 2 + from_z // 4)
         return ((d_hi * 4 + d_x) * 4 + from_z % 4) * part + src % part
 
-    dest = places(src // (16 * part), (src // part) % 2, (src // (2 * part)) % 8)
+    slot = (src // (2 * part)) % 8
+    step = sum(jnp.where(slot == n, k, 0) for n, k in enumerate((0, 4, 1, 5, 7, 3, 2, 6)))
+    dest = places(src // (16 * part), (src // part) % 2, step)
     order = narrow(lax.broadcasted_iota(jnp.int32, (count, count), 0) == dest[None, :])
-    order_turned = narrow(lax.broadcasted_iota(jnp.int32, (count, count), 1) == dest[:, None])
     back = places(src // (16 * part), (src // (8 * part)) % 2, (src // part) % 8)
     undo = narrow(lax.broadcasted_iota(jnp.int32, (count, count), 1) == back[:, None])
 
@@ -243,17 +291,18 @@
     far = jnp.concatenate(quarters[2:], axis=1)
 
     def gather_tokens(mine, other):
-        piece = jnp.stack([mine, send(other, y_hi=1)])
-        piece4 = jnp.stack([send(mine, z=4), send(other, y_hi=1, z=4)])
-        pair = jnp.stack([piece, piece4])
+        pair, piece = join(
+            [mine, send(other, y_hi=1), send(mine, z=4), send(other, y_hi=1, z=4)],
+            [4 * part, 2 * part],
+        )
         one, seven = send(pair, z=1), send(pair, z=-1)
         two, six = send(piece, z=2), send(piece, z=-2)
-        line = jnp.stack([piece, one[0], two, seven[1], piece4, one[1], six, seven[0]])
-        flat = jnp.stack([line, send(line, y_lo=1)]).reshape(count, 2 * feats)
-        return narrow(dot(order, flat, (1, 0))), narrow(dot(flat, order_turned, (0, 0)))
-
-    def project(tok):
-        got = send(gate_far(tok, gate_w), y_hi=1)
+        (line,) = join([pair, one, seven, two, six], [16 * part])
+        return line
+
+    def project(tok, gate_w, up_w):
+        first = gate_far(tok, gate_w)
+        got = send(first, y_hi=1)
         blocks = up_blocks(tok, up_w)
         ups = [send(blocks[k], x=k) for k in (1, 2, 3)]
         up = narrow(sum((wide(u) for u in ups), wide(blocks[0])))
@@ -311,15 +360,16 @@
             )
         return jnp.concatenate(ordered, axis=1), *beside
 
-    tok, turned = gather_tokens(near, far)
-    gate_pre, up_pre = project(tok)
+    line = gather_tokens(near, far)
+    tok = place(line, send(line, y_lo=1), order)
+    gate_pre, up_pre = project(tok, gate_w, up_w)
     hidden, grad_gate, grad_up = activate(gate_pre, up_pre, grad_hidden)
     gates, far_gates, ups = gather_grads(grad_gate, grad_up)
-    own_turned, other_turned = turned[:feats], send(turned[feats:], core=1)
+    parts = token_grads(gates, far_gates, ups, undo, gate_w, up_w)
     gates_too, far_too, ups_too = send(gates, core=1), send(far_gates, core=1), send(ups, core=1)
-    parts = token_grads(gates, far_gates, ups, undo, gate_w, up_w)
-    grad_wgate = weight_grad(own_turned, other_turned, [gates, far_gates, gates_too, far_too])
-    grad_wup = weight_grad(own_turned, other_turned, [ups, ups_too])
+    tok_too = send(tok[1], core=1)
+    grad_wgate = weight_grad(tok[0], tok_too, [gates, far_gates, gates_too, far_too])
+    grad_wup = weight_grad(tok[0], tok_too, [ups, ups_too])
     grad_tokens, grad_wgate, grad_wup = sum_tokens(parts, (grad_wgate, grad_wup))
     return (hidden, grad_tokens, grad_wgate, grad_wup)
 

time: 163 us -> 162 us (level)
  Pallas kernels: 16.5 us -> 22.7 us
  local copies, waits for them, and re-layouts: 5.53 us -> 0.94 us
  other arithmetic: 5.47 us -> 3.02 us
    pallas_call x3 -> x6, Pallas kernels: 4.47 us -> 8.83 us  [the longest x1 3.84 us: up_blocks(): call(up_kernel, 2, [half, half, whole(shape), whole(shape)], [pl.BlockSpe...]
    unnamed x11 -> x6, local copies, waits for them, and re-layouts: 3.89 us -> 0.02 us
  transfers between devices with their start and end apart: 38 -> 38, of which waited for: 19 -> 20; matrix products, arithmetic and copies ran while one was open for 6% -> 1% of each run, Pallas kernels for 10% -> 14%
where the time goes in v1:
time: 162 us
  waiting for transfers between devices  78.5 us (48%)
  starting transfers between devices  55.6 us (34%)
  Pallas kernels  22.7 us (14%)
  other arithmetic  3.02 us (2%)
    ppermute x38, waiting for transfers between devices, send(): lax.ppermute(array, AXES, permutation(lambda a, b, c, d, e: (a ^ x, b ^ y...  78.5 us
    ppermute x38, starting transfers between devices, send(): lax.ppermute(array, AXES, permutation(lambda a, b, c, d, e: (a ^ x, b ^ y...  55.6 us
    pallas_call x2, Pallas kernels, weight_grad(): call(weight_grad_kernel, 2, [side, side] + [whole(g.shape) for g in grads...  7.26 us
    pallas_call x1, Pallas kernels, token_grads(): call(token_grad_kernel, 2, [whole(gates.shape), whole(gates.shape), whole...  6.62 us
    pallas_call x1, Pallas kernels, up_blocks(): call(up_kernel, 2, [half, half, whole(shape), whole(shape)], [pl.BlockSpe...  3.84 us
  transfers between devices with their start and end apart: 38, of which 20 were waited for; matrix products, arithmetic and copies ran while one was open for 1% of the time, Pallas kernels for 14%

profile of v1, /device:TPU:2, one launch (start us, length us, event | category | flops | bytes accessed | tf_op | source)
XLA Modules:
  0.0 161.6 jit_solution(16288758792894431861)
XLA Ops:
  2.0 3.3 %collective-permute-start = (bf16[16,1024]{1,0:T(8,128)(2,1)S(1)}, bf16[16,1024]{1,0:T(8,128)(2,1)S(1)}, u32[]{:S(2)}, u32[]{:S(2)}) collective-permute-start(bf16[16,1024]{1,0:T(8,128)(2,1)S(1)} %pad_maximum_fusion.8), channel_id=1, source_target_pairs={{0,128},{1,129},{2,130},{3,131},{4,132},{5,133},{6,134},{7,135},{8... | collective-permute-start | bytes 98312 | tf_op jit(solution)/shard_map/ppermute | solution.py:26
  5.3 7.2 %collective-permute-start.1 = (bf16[16,1024]{1,0:T(8,128)(2,1)S(1)}, bf16[16,1024]{1,0:T(8,128)(2,1)S(1)}, u32[]{:S(2)}, u32[]{:S(2)}) collective-permute-start(bf16[16,1024]{1,0:T(8,128)(2,1)S(1)} %pad_maximum_fusion.7.refs_0_), channel_id=1, source_target_pairs={{0,16},{1,17},{2,18},{3,19},{4,20},{5,21},{6,22},{7,23},{8,24},{9,... | collective-permute-start | bytes 98312 | tf_op jit(solution)/shard_map/ppermute | solution.py:26
  12.5 1.9 %collective-permute-done.1.refs_2_ = bf16[16,1024]{1,0:T(8,128)(2,1)S(1)} collective-permute-done((bf16[16,1024]{1,0:T(8,128)(2,1)S(1)}, bf16[16,1024]{1,0:T(8,128)(2,1)S(1)}, u32[]{:S(2)}, u32[]{:S(2)}) %collective-permute-start.1) | collective-permute-done | bytes 32800 | tf_op jit(solution)/shard_map/ppermute | solution.py:26
  14.4 8.3 %collective-permute-done.2.refs_3_ = bf16[16,1024]{1,0:T(8,128)(2,1)S(1)} collective-permute-done((bf16[16,1024]{1,0:T(8,128)(2,1)S(1)}, bf16[16,1024]{1,0:T(8,128)(2,1)S(1)}, u32[]{:S(2)}, u32[]{:S(2)}) %collective-permute-start.2) | collective-permute-done | bytes 32800 | tf_op jit(solution)/shard_map/ppermute | solution.py:26
  25.3 2.2 %collective-permute-start.4 = (bf16[64,1024]{1,0:T(8,128)(2,1)S(1)}, bf16[64,1024]{1,0:T(8,128)(2,1)S(1)}, u32[]{:S(2)}, u32[]{:S(2)}) collective-permute-start(bf16[64,1024]{1,0:T(8,128)(2,1)S(1)} %get-tuple-element.25.refs_0_), channel_id=1, source_target_pairs={{0,28},{1,29},{2,30},{3,31},{4,0},{5,1},{6,2},{7,3},{8,4},{9,5},{1... | collective-permute-start | bytes 393224 | tf_op jit(solution)/shard_map/ppermute | solution.py:26
  27.5 2.0 %collective-permute-done.5.refs_3_ = bf16[32,1024]{1,0:T(8,128)(2,1)S(1)} collective-permute-done((bf16[32,1024]{1,0:T(8,128)(2,1)S(1)}, bf16[32,1024]{1,0:T(8,128)(2,1)S(1)}, u32[]{:S(2)}, u32[]{:S(2)}) %collective-permute-start.5) | collective-permute-done | bytes 65568 | tf_op jit(solution)/shard_map/ppermute | solution.py:26
  29.6 5.2 %collective-permute-done.6.refs_4_ = bf16[32,1024]{1,0:T(8,128)(2,1)S(1)} collective-permute-done((bf16[32,1024]{1,0:T(8,128)(2,1)S(1)}, bf16[32,1024]{1,0:T(8,128)(2,1)S(1)}, u32[]{:S(2)}, u32[]{:S(2)}) %collective-permute-start.6) | collective-permute-done | bytes 65568 | tf_op jit(solution)/shard_map/ppermute | solution.py:26
  36.5 9.4 %collective-permute-done.7.second = bf16[256,1024]{1,0:T(8,128)(2,1)} collective-permute-done((bf16[256,1024]{1,0:T(8,128)(2,1)}, bf16[256,1024]{1,0:T(8,128)(2,1)}, u32[]{:S(2)}, u32[]{:S(2)}) %collective-permute-start.7) | collective-permute-done | bytes 524320 | tf_op jit(solution)/shard_map/ppermute | solution.py:26
  45.8 1.9 %shard_map.77 = (bf16[512,512]{1,0:T(8,128)(2,1)S(1)}, bf16[512,512]{1,0:T(8,128)(2,1)S(1)}) custom-call(bf16[256,1024]{1,0:T(8,128)(2,1)} %shard_map.76.first, bf16[256,1024]{1,0:T(8,128)(2,1)} %collective-permute-done.7.second, bf16[512,512]{1,0:T(8,128)(2,1)S(1)} %fusion.order), custom_call_target="tpu_custom_call" | custom-call | flops 1048576 | bytes 1048576 | tf_op jit(solution)/shard_map/pallas_call | solution.py:180
  47.8 3.8 %shard_map.80 = (bf16[2,64,1664]{2,1,0:T(8,128)(2,1)S(1)}, bf16[2,64,1664]{2,1,0:T(8,128)(2,1)S(1)}, bf16[2,64,1664]{2,1,0:T(8,128)(2,1)S(1)}, bf16[2,64,1664]{2,1,0:T(8,128)(2,1)S(1)}) custom-call(bf16[512,512]{1,0:T(8,128)(2,1)S(1)} %get-tuple-element.27.near.refs_0_, bf16[512,512]{1,0:T(8,128)(2,1)S(1)} %get-tuple-element.28.distant, ...), custom_call_target="tpu_custom_call" | custom-call | flops 1048576 | bytes 1048576 | tf_op jit(solution)/shard_map/pallas_call | solution.py:135
  58.3 9.5 %collective-permute-done.16 = bf16[2,64,1664]{2,1,0:T(8,128)(2,1)S(1)} collective-permute-done((bf16[2,64,1664]{2,1,0:T(8,128)(2,1)S(1)}, bf16[2,64,1664]{2,1,0:T(8,128)(2,1)S(1)}, u32[]{:S(2)}, u32[]{:S(2)}) %collective-permute-start.16) | collective-permute-done | bytes 426016 | tf_op jit(solution)/shard_map/ppermute | solution.py:26
  69.9 2.2 %collective-permute-start.17 = (bf16[64,1664]{1,0:T(8,128)(2,1)S(1)}, bf16[64,1664]{1,0:T(8,128)(2,1)S(1)}, u32[]{:S(2)}, u32[]{:S(2)}) collective-permute-start(bf16[64,1664]{1,0:T(8,128)(2,1)S(1)} %slice_bitcast_fusion), channel_id=1, source_target_pairs={{0,128},{1,129},{2,130},{3,131},{4,132},{5,133},{6,134},{7,135},{8... | collective-permute-start | bytes 638984 | tf_op jit(solution)/shard_map/ppermute | solution.py:26
  72.1 4.0 %collective-permute-done.9.far = bf16[256,1664]{1,0:T(8,128)(2,1)S(1)} collective-permute-done((bf16[256,1664]{1,0:T(8,128)(2,1)S(1)}, bf16[256,1664]{1,0:T(8,128)(2,1)S(1)}, u32[]{:S(2)}, u32[]{:S(2)}) %collective-permute-start.9) | collective-permute-done | bytes 852000 | tf_op jit(solution)/shard_map/ppermute | solution.py:26
  83.1 3.1 %collective-permute-done.11 = bf16[64,1664]{1,0:T(8,128)(2,1)S(1)} collective-permute-done((bf16[64,1664]{1,0:T(8,128)(2,1)S(1)}, bf16[64,1664]{1,0:T(8,128)(2,1)S(1)}, u32[]{:S(2)}, u32[]{:S(2)}) %collective-permute-start.11) | collective-permute-done | bytes 213024 | tf_op jit(solution)/shard_map/ppermute | solution.py:26
  86.2 2.5 %collective-permute-done.10 = bf16[64,1664]{1,0:T(8,128)(2,1)S(1)} collective-permute-done((bf16[64,1664]{1,0:T(8,128)(2,1)S(1)}, bf16[64,1664]{1,0:T(8,128)(2,1)S(1)}, u32[]{:S(2)}, u32[]{:S(2)}) %collective-permute-start.10) | collective-permute-done | bytes 213024 | tf_op jit(solution)/shard_map/ppermute | solution.py:26
  91.0 1.9 %collective-permute-start.20 = (bf16[64,1664]{1,0:T(8,128)(2,1)S(1)}, bf16[64,1664]{1,0:T(8,128)(2,1)S(1)}, u32[]{:S(2)}, u32[]{:S(2)}) collective-permute-start(bf16[64,1664]{1,0:T(8,128)(2,1)S(1)} %get-tuple-element.46), channel_id=1, source_target_pairs={{0,3},{1,2},{2,1},{3,0},{4,7},{5,6},{6,5},{7,4},{8,11},{9,10},{10,... | collective-permute-start | bytes 638984 | tf_op jit(solution)/shard_map/ppermute | solution.py:26
  92.9 2.2 %collective-permute-start.18 = (bf16[64,1664]{1,0:T(8,128)(2,1)S(1)}, bf16[64,1664]{1,0:T(8,128)(2,1)S(1)}, u32[]{:S(2)}, u32[]{:S(2)}) collective-permute-start(bf16[64,1664]{1,0:T(8,128)(2,1)S(1)} %get-tuple-element.46), channel_id=1, source_target_pairs={{0,1},{1,0},{2,3},{3,2},{4,5},{5,4},{6,7},{7,6},{8,9},{9,8},{10,11... | collective-permute-start | bytes 638984 | tf_op jit(solution)/shard_map/ppermute | solution.py:26
  95.1 2.8 %collective-permute-done.22 = bf16[64,1664]{1,0:T(8,128)(2,1)S(1)} collective-permute-done((bf16[64,1664]{1,0:T(8,128)(2,1)S(1)}, bf16[64,1664]{1,0:T(8,128)(2,1)S(1)}, u32[]{:S(2)}, u32[]{:S(2)}) %collective-permute-start.22) | collective-permute-done | bytes 213024 | tf_op jit(solution)/shard_map/ppermute | solution.py:26
  98.0 2.5 %collective-permute-start.25 = (bf16[2,64,1664]{2,1,0:T(8,128)(2,1)S(1)}, bf16[2,64,1664]{2,1,0:T(8,128)(2,1)S(1)}, u32[]{:S(2)}, u32[]{:S(2)}) collective-permute-start(bf16[2,64,1664]{2,1,0:T(8,128)(2,1)S(1)} %get-tuple-element.56), channel_id=1, source_target_pairs={{0,3},{1,2},{2,1},{3,0},{4,7},{5,6},{6,5},{7,4},{8,11},{9,10},{10,... | collective-permute-start | bytes 1277960 | tf_op jit(solution)/shard_map/ppermute | solution.py:26
  100.5 3.8 %collective-permute-done.20 = bf16[64,1664]{1,0:T(8,128)(2,1)S(1)} collective-permute-done((bf16[64,1664]{1,0:T(8,128)(2,1)S(1)}, bf16[64,1664]{1,0:T(8,128)(2,1)S(1)}, u32[]{:S(2)}, u32[]{:S(2)}) %collective-permute-start.20) | collective-permute-done | bytes 213024 | tf_op jit(solution)/shard_map/ppermute | solution.py:26
  106.1 2.1 %collective-permute-start.21 = (bf16[256,1664]{1,0:T(8,128)(2,1)S(1)}, bf16[256,1664]{1,0:T(8,128)(2,1)S(1)}, u32[]{:S(2)}, u32[]{:S(2)}) collective-permute-start(bf16[256,1664]{1,0:T(8,128)(2,1)S(1)} %pad_maximum_fusion.1.gates.refs_2_), channel_id=1, source_target_pairs={{0,128},{1,129},{2,130},{3,131},{4,132},{5,133},{6,134},{7,135},{8... | collective-permute-start | bytes 2555912 | tf_op jit(solution)/shard_map/ppermute | solution.py:26
  108.2 5.3 %collective-permute-done.25 = bf16[2,64,1664]{2,1,0:T(8,128)(2,1)S(1)} collective-permute-done((bf16[2,64,1664]{2,1,0:T(8,128)(2,1)S(1)}, bf16[2,64,1664]{2,1,0:T(8,128)(2,1)S(1)}, u32[]{:S(2)}, u32[]{:S(2)}) %collective-permute-start.25) | collective-permute-done | bytes 426016 | tf_op jit(solution)/shard_map/ppermute | solution.py:26
  116.0 4.4 %collective-permute-done.21.far_gates.refs_3_ = bf16[256,1664]{1,0:T(8,128)(2,1)S(1)} collective-permute-done((bf16[256,1664]{1,0:T(8,128)(2,1)S(1)}, bf16[256,1664]{1,0:T(8,128)(2,1)S(1)}, u32[]{:S(2)}, u32[]{:S(2)}) %collective-permute-start.21) | collective-permute-done | bytes 852000 | tf_op jit(solution)/shard_map/ppermute | solution.py:26
  121.1 6.6 %shard_map.81 = (bf16[128,1024]{1,0:T(8,128)(2,1)S(1)}, bf16[128,1024]{1,0:T(8,128)(2,1)S(1)}, bf16[128,1024]{1,0:T(8,128)(2,1)S(1)}, bf16[128,1024]{1,0:T(8,128)(2,1)S(1)}) custom-call(bf16[256,1664]{1,0:T(8,128)(2,1)S(1)} %pad_maximum_fusion.1.gates.refs_2_, bf16[256,1664]{1,0:T(8,128)(2,1)S(1)} %collective-permute-done.21.far_gates.refs_3_, ...), custom_call_target="tpu_custom_call" | custom-call | flops 1048576 | bytes 1048576 | tf_op jit(solution)/shard_map/pallas_call | solution.py:219
  127.7 2.1 %collective-permute-start.26 = (bf16[128,1024]{1,0:T(8,128)(2,1)S(1)}, bf16[128,1024]{1,0:T(8,128)(2,1)S(1)}, u32[]{:S(2)}, u32[]{:S(2)}) collective-permute-start(bf16[128,1024]{1,0:T(8,128)(2,1)S(1)} %get-tuple-element.38), channel_id=1, source_target_pairs={{0,128},{1,129},{2,130},{3,131},{4,132},{5,133},{6,134},{7,135},{8... | collective-permute-start | bytes 786440 | tf_op jit(solution)/shard_map/ppermute | solution.py:26
  129.8 2.1 %collective-permute-start.28 = (bf16[128,1024]{1,0:T(8,128)(2,1)S(1)}, bf16[128,1024]{1,0:T(8,128)(2,1)S(1)}, u32[]{:S(2)}, u32[]{:S(2)}) collective-permute-start(bf16[128,1024]{1,0:T(8,128)(2,1)S(1)} %get-tuple-element.40), channel_id=1, source_target_pairs={{0,160},{1,161},{2,162},{3,163},{4,164},{5,165},{6,166},{7,167},{8... | collective-permute-start | bytes 786440 | tf_op jit(solution)/shard_map/ppermute | solution.py:26
  131.9 3.6 %shard_map.82 = f32[512,1664]{1,0:T(8,128)} custom-call(bf16[512,512]{1,0:T(8,128)(2,1)S(1)} %get-tuple-element.27.near.refs_0_, bf16[512,512]{1,0:T(8,128)(2,1)S(1)} %collective-permute-done.29.refs_1_, bf16[256,1664]{1,0:T(8,128)(2,1)S(1)} %pad_maximum_fusion.1.gates.refs_2_, bf16[256,1664]{1,0:T(8,128)(2,1)S(1)} %collective-permute-done.21.far_gates.refs_3_, ...), custom_call_target="tpu_custom_call" | custom-call | flops 1048576 | bytes 1048576 | tf_op jit(solution)/shard_map/pallas_call | solution.py:248
  135.5 3.6 %shard_map.83 = f32[512,1664]{1,0:T(8,128)} custom-call(bf16[512,512]{1,0:T(8,128)(2,1)S(1)} %get-tuple-element.27.near.refs_0_, bf16[512,512]{1,0:T(8,128)(2,1)S(1)} %collective-permute-done.29.refs_1_, bf16[512,1664]{1,0:T(8,128)(2,1)S(1)} %bitcast.43, bf16[512,1664]{1,0:T(8,128)(2,1)S(1)} %collective-permute-done.32.refs_3_), custom_call_target="tpu_custom_call" | custom-call | flops 1048576 | bytes 1048576 | tf_op jit(solution)/shard_map/pallas_call | solution.py:248
  139.1 2.3 %collective-permute-done.27 = bf16[128,1024]{1,0:T(8,128)(2,1)S(1)} collective-permute-done((bf16[128,1024]{1,0:T(8,128)(2,1)S(1)}, bf16[128,1024]{1,0:T(8,128)(2,1)S(1)}, u32[]{:S(2)}, u32[]{:S(2)}) %collective-permute-start.27) | collective-permute-done | bytes 262176 | tf_op jit(solution)/shard_map/ppermute | solution.py:26
  144.7 3.1 %collective-permute-start.33 = (bf16[2,2,16,1024]{3,2,1,0:T(8,128)(2,1)S(1)}, bf16[2,2,16,1024]{3,2,1,0:T(8,128)(2,1)S(1)}, u32[]{:S(2)}, u32[]{:S(2)}) collective-permute-start(bf16[2,2,16,1024]{3,2,1,0:T(8,128)(2,1)S(1)} %pad_maximum_fusion.3), channel_id=1, source_target_pairs={{0,28},{1,29},{2,30},{3,31},{4,0},{5,1},{6,2},{7,3},{8,4},{9,5},{1... | collective-permute-start | bytes 393224 | tf_op jit(solution)/shard_map/ppermute | solution.py:26
  147.8 4.1 %collective-permute-start.35 = (bf16[2,16,1024]{2,1,0:T(8,128)(2,1)S(1)}, bf16[2,16,1024]{2,1,0:T(8,128)(2,1)S(1)}, u32[]{:S(2)}, u32[]{:S(2)}) collective-permute-start(bf16[2,16,1024]{2,1,0:T(8,128)(2,1)S(1)} %get-tuple-element.49), channel_id=1, source_target_pairs={{0,24},{1,25},{2,26},{3,27},{4,28},{5,29},{6,30},{7,31},{8,0},{9,1... | collective-permute-start | bytes 196616 | tf_op jit(solution)/shard_map/ppermute | solution.py:26
  155.0 5.9 %collective-permute-done.37 = bf16[2,16,1024]{2,1,0:T(8,128)(2,1)S(1)} collective-permute-done((bf16[2,16,1024]{2,1,0:T(8,128)(2,1)S(1)}, bf16[2,16,1024]{2,1,0:T(8,128)(2,1)S(1)}, u32[]{:S(2)}, u32[]{:S(2)}) %collective-permute-start.37) | collective-permute-done | bytes 65568 | tf_op jit(solution)/shard_map/ppermute | solution.py:26
  (83 shorter events, 35.9 us)
Async XLA Ops:
  0.6 47.1 %collective-permute-start.13 = (bf16[512,1664]{1,0:T(8,128)(2,1)}, bf16[512,1664]{1,0:T(8,128)(2,1)}, u32[]{:S(2)}, u32[]{:S(2)}) collective-permute-start(bf16[512,1664]{1,0:T(8,128)(2,1)} %wu0.1), channel_id=1, source_target_pairs={{0,64},{1,65},{2,66},{3,67},{4,68},{5,69},{6,70},{7,71},{8,72},{9,... | collective-permute-start | bytes 5111816 | tf_op jit(solution)/shard_map/ppermute | solution.py:26
  0.7 55.1 %collective-permute-start.8 = (bf16[512,1664]{1,0:T(8,128)(2,1)}, bf16[512,1664]{1,0:T(8,128)(2,1)S(1)}, u32[]{:S(2)}, u32[]{:S(2)}) collective-permute-start(bf16[512,1664]{1,0:T(8,128)(2,1)} %wg0.1), channel_id=1, source_target_pairs={{0,64},{1,65},{2,66},{3,67},{4,68},{5,69},{6,70},{7,71},{8,72},{9,... | collective-permute-start | bytes 5111816 | tf_op jit(solution)/shard_map/ppermute | solution.py:26
  2.0 10.5 %collective-permute-start = (bf16[16,1024]{1,0:T(8,128)(2,1)S(1)}, bf16[16,1024]{1,0:T(8,128)(2,1)S(1)}, u32[]{:S(2)}, u32[]{:S(2)}) collective-permute-start(bf16[16,1024]{1,0:T(8,128)(2,1)S(1)} %pad_maximum_fusion.8), channel_id=1, source_target_pairs={{0,128},{1,129},{2,130},{3,131},{4,132},{5,133},{6,134},{7,135},{8... | collective-permute-start | bytes 98312 | tf_op jit(solution)/shard_map/ppermute | solution.py:26
  5.3 9.1 %collective-permute-start.1 = (bf16[16,1024]{1,0:T(8,128)(2,1)S(1)}, bf16[16,1024]{1,0:T(8,128)(2,1)S(1)}, u32[]{:S(2)}, u32[]{:S(2)}) collective-permute-start(bf16[16,1024]{1,0:T(8,128)(2,1)S(1)} %pad_maximum_fusion.7.refs_0_), channel_id=1, source_target_pairs={{0,16},{1,17},{2,18},{3,19},{4,20},{5,21},{6,22},{7,23},{8,24},{9,... | collective-permute-start | bytes 98312 | tf_op jit(solution)/shard_map/ppermute | solution.py:26
  12.5 10.2 %collective-permute-start.2 = (bf16[16,1024]{1,0:T(8,128)(2,1)S(1)}, bf16[16,1024]{1,0:T(8,128)(2,1)S(1)}, u32[]{:S(2)}, u32[]{:S(2)}) collective-permute-start(bf16[16,1024]{1,0:T(8,128)(2,1)S(1)} %pad_maximum_fusion.8), channel_id=1, source_target_pairs={{0,144},{1,145},{2,146},{3,147},{4,148},{5,149},{6,150},{7,151},{8... | collective-permute-start | bytes 98312 | tf_op jit(solution)/shard_map/ppermute | solution.py:26
  24.3 10.4 %collective-permute-start.3 = (bf16[64,1024]{1,0:T(8,128)(2,1)S(1)}, bf16[64,1024]{1,0:T(8,128)(2,1)S(1)}, u32[]{:S(2)}, u32[]{:S(2)}) collective-permute-start(bf16[64,1024]{1,0:T(8,128)(2,1)S(1)} %get-tuple-element.25.refs_0_), channel_id=1, source_target_pairs={{0,4},{1,5},{2,6},{3,7},{4,8},{5,9},{6,10},{7,11},{8,12},{9,13},{1... | collective-permute-start | bytes 393224 | tf_op jit(solution)/shard_map/ppermute | solution.py:26
  25.3 9.4 %collective-permute-start.4 = (bf16[64,1024]{1,0:T(8,128)(2,1)S(1)}, bf16[64,1024]{1,0:T(8,128)(2,1)S(1)}, u32[]{:S(2)}, u32[]{:S(2)}) collective-permute-start(bf16[64,1024]{1,0:T(8,128)(2,1)S(1)} %get-tuple-element.25.refs_0_), channel_id=1, source_target_pairs={{0,28},{1,29},{2,30},{3,31},{4,0},{5,1},{6,2},{7,3},{8,4},{9,5},{1... | collective-permute-start | bytes 393224 | tf_op jit(solution)/shard_map/ppermute | solution.py:26
  35.6 10.3 %collective-permute-start.7 = (bf16[256,1024]{1,0:T(8,128)(2,1)}, bf16[256,1024]{1,0:T(8,128)(2,1)}, u32[]{:S(2)}, u32[]{:S(2)}) collective-permute-start(bf16[256,1024]{1,0:T(8,128)(2,1)} %shard_map.76.first), channel_id=1, source_target_pairs={{0,32},{1,33},{2,34},{3,35},{4,36},{5,37},{6,38},{7,39},{8,40},{9,... | collective-permute-start | bytes 1572872 | tf_op jit(solution)/shard_map/ppermute | solution.py:26
  51.6 16.1 %collective-permute-start.16 = (bf16[2,64,1664]{2,1,0:T(8,128)(2,1)S(1)}, bf16[2,64,1664]{2,1,0:T(8,128)(2,1)S(1)}, u32[]{:S(2)}, u32[]{:S(2)}) collective-permute-start(bf16[2,64,1664]{2,1,0:T(8,128)(2,1)S(1)} %get-tuple-element.36), channel_id=1, source_target_pairs={{0,3},{1,2},{2,1},{3,0},{4,7},{5,6},{6,5},{7,4},{8,11},{9,10},{10,... | collective-permute-start | bytes 1277960 | tf_op jit(solution)/shard_map/ppermute | solution.py:26
  53.2 14.6 %collective-permute-start.15 = (bf16[2,64,1664]{2,1,0:T(8,128)(2,1)S(1)}, bf16[2,64,1664]{2,1,0:T(8,128)(2,1)S(1)}, u32[]{:S(2)}, u32[]{:S(2)}) collective-permute-start(bf16[2,64,1664]{2,1,0:T(8,128)(2,1)S(1)} %get-tuple-element.35), channel_id=1, source_target_pairs={{0,2},{1,3},{2,0},{3,1},{4,6},{5,7},{6,4},{7,5},{8,10},{9,11},{10,... | collective-permute-start | bytes 1277960 | tf_op jit(solution)/shard_map/ppermute | solution.py:26
  54.3 15.3 %collective-permute-start.14 = (bf16[2,64,1664]{2,1,0:T(8,128)(2,1)S(1)}, bf16[2,64,1664]{2,1,0:T(8,128)(2,1)S(1)}, u32[]{:S(2)}, u32[]{:S(2)}) collective-permute-start(bf16[2,64,1664]{2,1,0:T(8,128)(2,1)S(1)} %get-tuple-element.34), channel_id=1, source_target_pairs={{0,1},{1,0},{2,3},{3,2},{4,5},{5,4},{6,7},{7,6},{8,9},{9,8},{10,11... | collective-permute-start | bytes 1277960 | tf_op jit(solution)/shard_map/ppermute | solution.py:26
  56.9 19.1 %collective-permute-start.9 = (bf16[256,1664]{1,0:T(8,128)(2,1)S(1)}, bf16[256,1664]{1,0:T(8,128)(2,1)S(1)}, u32[]{:S(2)}, u32[]{:S(2)}) collective-permute-start(bf16[256,1664]{1,0:T(8,128)(2,1)S(1)} %shard_map.78), channel_id=1, source_target_pairs={{0,128},{1,129},{2,130},{3,131},{4,132},{5,133},{6,134},{7,135},{8... | collective-permute-start | bytes 2555912 | tf_op jit(solution)/shard_map/ppermute | solution.py:26
  69.9 11.4 %collective-permute-start.17 = (bf16[64,1664]{1,0:T(8,128)(2,1)S(1)}, bf16[64,1664]{1,0:T(8,128)(2,1)S(1)}, u32[]{:S(2)}, u32[]{:S(2)}) collective-permute-start(bf16[64,1664]{1,0:T(8,128)(2,1)S(1)} %slice_bitcast_fusion), channel_id=1, source_target_pairs={{0,128},{1,129},{2,130},{3,131},{4,132},{5,133},{6,134},{7,135},{8... | collective-permute-start | bytes 638984 | tf_op jit(solution)/shard_map/ppermute | solution.py:26
  78.7 7.5 %collective-permute-start.11 = (bf16[64,1664]{1,0:T(8,128)(2,1)S(1)}, bf16[64,1664]{1,0:T(8,128)(2,1)S(1)}, u32[]{:S(2)}, u32[]{:S(2)}) collective-permute-start(bf16[64,1664]{1,0:T(8,128)(2,1)S(1)} %get-tuple-element.31), channel_id=1, source_target_pairs={{0,2},{1,3},{2,0},{3,1},{4,6},{5,7},{6,4},{7,5},{8,10},{9,11},{10,... | collective-permute-start | bytes 638984 | tf_op jit(solution)/shard_map/ppermute | solution.py:26
  79.7 8.9 %collective-permute-start.10 = (bf16[64,1664]{1,0:T(8,128)(2,1)S(1)}, bf16[64,1664]{1,0:T(8,128)(2,1)S(1)}, u32[]{:S(2)}, u32[]{:S(2)}) collective-permute-start(bf16[64,1664]{1,0:T(8,128)(2,1)S(1)} %get-tuple-element.30), channel_id=1, source_target_pairs={{0,1},{1,0},{2,3},{3,2},{4,5},{5,4},{6,7},{7,6},{8,9},{9,8},{10,11... | collective-permute-start | bytes 638984 | tf_op jit(solution)/shard_map/ppermute | solution.py:26
  89.7 8.2 %collective-permute-start.22 = (bf16[64,1664]{1,0:T(8,128)(2,1)S(1)}, bf16[64,1664]{1,0:T(8,128)(2,1)S(1)}, u32[]{:S(2)}, u32[]{:S(2)}) collective-permute-start(bf16[64,1664]{1,0:T(8,128)(2,1)S(1)} %get-tuple-element.48), channel_id=1, source_target_pairs={{0,128},{1,129},{2,130},{3,131},{4,132},{5,133},{6,134},{7,135},{8... | collective-permute-start | bytes 638984 | tf_op jit(solution)/shard_map/ppermute | solution.py:26
  91.0 13.3 %collective-permute-start.20 = (bf16[64,1664]{1,0:T(8,128)(2,1)S(1)}, bf16[64,1664]{1,0:T(8,128)(2,1)S(1)}, u32[]{:S(2)}, u32[]{:S(2)}) collective-permute-start(bf16[64,1664]{1,0:T(8,128)(2,1)S(1)} %get-tuple-element.46), channel_id=1, source_target_pairs={{0,3},{1,2},{2,1},{3,0},{4,7},{5,6},{6,5},{7,4},{8,11},{9,10},{10,... | collective-permute-start | bytes 638984 | tf_op jit(solution)/shard_map/ppermute | solution.py:26
  92.9 13.1 %collective-permute-start.19 = (bf16[64,1664]{1,0:T(8,128)(2,1)S(1)}, bf16[64,1664]{1,0:T(8,128)(2,1)S(1)}, u32[]{:S(2)}, u32[]{:S(2)}) collective-permute-start(bf16[64,1664]{1,0:T(8,128)(2,1)S(1)} %get-tuple-element.46), channel_id=1, source_target_pairs={{0,2},{1,3},{2,0},{3,1},{4,6},{5,7},{6,4},{7,5},{8,10},{9,11},{10,... | collective-permute-start | bytes 638984 | tf_op jit(solution)/shard_map/ppermute | solution.py:26
  92.9 13.1 %collective-permute-start.18 = (bf16[64,1664]{1,0:T(8,128)(2,1)S(1)}, bf16[64,1664]{1,0:T(8,128)(2,1)S(1)}, u32[]{:S(2)}, u32[]{:S(2)}) collective-permute-start(bf16[64,1664]{1,0:T(8,128)(2,1)S(1)} %get-tuple-element.46), channel_id=1, source_target_pairs={{0,1},{1,0},{2,3},{3,2},{4,5},{5,4},{6,7},{7,6},{8,9},{9,8},{10,11... | collective-permute-start | bytes 638984 | tf_op jit(solution)/shard_map/ppermute | solution.py:26
  98.0 15.5 %collective-permute-start.25 = (bf16[2,64,1664]{2,1,0:T(8,128)(2,1)S(1)}, bf16[2,64,1664]{2,1,0:T(8,128)(2,1)S(1)}, u32[]{:S(2)}, u32[]{:S(2)}) collective-permute-start(bf16[2,64,1664]{2,1,0:T(8,128)(2,1)S(1)} %get-tuple-element.56), channel_id=1, source_target_pairs={{0,3},{1,2},{2,1},{3,0},{4,7},{5,6},{6,5},{7,4},{8,11},{9,10},{10,... | collective-permute-start | bytes 1277960 | tf_op jit(solution)/shard_map/ppermute | solution.py:26
  100.5 12.9 %collective-permute-start.24 = (bf16[2,64,1664]{2,1,0:T(8,128)(2,1)S(1)}, bf16[2,64,1664]{2,1,0:T(8,128)(2,1)S(1)}, u32[]{:S(2)}, u32[]{:S(2)}) collective-permute-start(bf16[2,64,1664]{2,1,0:T(8,128)(2,1)S(1)} %get-tuple-element.56), channel_id=1, source_target_pairs={{0,2},{1,3},{2,0},{3,1},{4,6},{5,7},{6,4},{7,5},{8,10},{9,11},{10,... | collective-permute-start | bytes 1277960 | tf_op jit(solution)/shard_map/ppermute | solution.py:26
  104.3 10.6 %collective-permute-start.23 = (bf16[2,64,1664]{2,1,0:T(8,128)(2,1)S(1)}, bf16[2,64,1664]{2,1,0:T(8,128)(2,1)S(1)}, u32[]{:S(2)}, u32[]{:S(2)}) collective-permute-start(bf16[2,64,1664]{2,1,0:T(8,128)(2,1)S(1)} %get-tuple-element.56), channel_id=1, source_target_pairs={{0,1},{1,0},{2,3},{3,2},{4,5},{5,4},{6,7},{7,6},{8,9},{9,8},{10,11... | collective-permute-start | bytes 1277960 | tf_op jit(solution)/shard_map/ppermute | solution.py:26
  106.1 14.3 %collective-permute-start.21 = (bf16[256,1664]{1,0:T(8,128)(2,1)S(1)}, bf16[256,1664]{1,0:T(8,128)(2,1)S(1)}, u32[]{:S(2)}, u32[]{:S(2)}) collective-permute-start(bf16[256,1664]{1,0:T(8,128)(2,1)S(1)} %pad_maximum_fusion.1.gates.refs_2_), channel_id=1, source_target_pairs={{0,128},{1,129},{2,130},{3,131},{4,132},{5,133},{6,134},{7,135},{8... | collective-permute-start | bytes 2555912 | tf_op jit(solution)/shard_map/ppermute | solution.py:26
  115.4 20.1 %collective-permute-start.32 = (bf16[512,1664]{1,0:T(8,128)(2,1)S(1)}, bf16[512,1664]{1,0:T(8,128)(2,1)S(1)}, u32[]{:S(2)}, u32[]{:S(2)}) collective-permute-start(bf16[512,1664]{1,0:T(8,128)(2,1)S(1)} %bitcast.41), channel_id=1, source_target_pairs={{0,64},{1,65},{2,66},{3,67},{4,68},{5,69},{6,70},{7,71},{8,72},{9,... | collective-permute-start | bytes 5111816 | tf_op jit(solution)/shard_map/ppermute | solution.py:26
  115.5 14.3 %collective-permute-start.30 = (bf16[256,1664]{1,0:T(8,128)(2,1)S(1)}, bf16[256,1664]{1,0:T(8,128)(2,1)S(1)}, u32[]{:S(2)}, u32[]{:S(2)}) collective-permute-start(bf16[256,1664]{1,0:T(8,128)(2,1)S(1)} %pad_maximum_fusion.1.gates.refs_2_), channel_id=1, source_target_pairs={{0,64},{1,65},{2,66},{3,67},{4,68},{5,69},{6,70},{7,71},{8,72},{9,... | collective-permute-start | bytes 2555912 | tf_op jit(solution)/shard_map/ppermute | solution.py:26
  120.4 11.5 %collective-permute-start.31 = (bf16[256,1664]{1,0:T(8,128)(2,1)S(1)}, bf16[256,1664]{1,0:T(8,128)(2,1)S(1)}, u32[]{:S(2)}, u32[]{:S(2)}) collective-permute-start(bf16[256,1664]{1,0:T(8,128)(2,1)S(1)} %collective-permute-done.21.far_gates.refs_3_), channel_id=1, source_target_pairs={{0,64},{1,65},{2,66},{3,67},{4,68},{5,69},{6,70},{7,71},{8,72},{9,... | collective-permute-start | bytes 2555912 | tf_op jit(solution)/shard_map/ppermute | solution.py:26
  120.4 9.4 %collective-permute-start.29 = (bf16[512,512]{1,0:T(8,128)(2,1)S(1)}, bf16[512,512]{1,0:T(8,128)(2,1)S(1)}, u32[]{:S(2)}, u32[]{:S(2)}) collective-permute-start(bf16[512,512]{1,0:T(8,128)(2,1)S(1)} %get-tuple-element.28.distant), channel_id=1, source_target_pairs={{0,64},{1,65},{2,66},{3,67},{4,68},{5,69},{6,70},{7,71},{8,72},{9,... | collective-permute-start | bytes 1572872 | tf_op jit(solution)/shard_map/ppermute | solution.py:26
  127.7 11.5 %collective-permute-start.26 = (bf16[128,1024]{1,0:T(8,128)(2,1)S(1)}, bf16[128,1024]{1,0:T(8,128)(2,1)S(1)}, u32[]{:S(2)}, u32[]{:S(2)}) collective-permute-start(bf16[128,1024]{1,0:T(8,128)(2,1)S(1)} %get-tuple-element.38), channel_id=1, source_target_pairs={{0,128},{1,129},{2,130},{3,131},{4,132},{5,133},{6,134},{7,135},{8... | collective-permute-start | bytes 786440 | tf_op jit(solution)/shard_map/ppermute | solution.py:26
  129.8 11.7 %collective-permute-start.27 = (bf16[128,1024]{1,0:T(8,128)(2,1)S(1)}, bf16[128,1024]{1,0:T(8,128)(2,1)S(1)}, u32[]{:S(2)}, u32[]{:S(2)}) collective-permute-start(bf16[128,1024]{1,0:T(8,128)(2,1)S(1)} %get-tuple-element.39), channel_id=1, source_target_pairs={{0,32},{1,33},{2,34},{3,35},{4,36},{5,37},{6,38},{7,39},{8,40},{9,... | collective-permute-start | bytes 786440 | tf_op jit(solution)/shard_map/ppermute | solution.py:26
  129.8 13.3 %collective-permute-start.28 = (bf16[128,1024]{1,0:T(8,128)(2,1)S(1)}, bf16[128,1024]{1,0:T(8,128)(2,1)S(1)}, u32[]{:S(2)}, u32[]{:S(2)}) collective-permute-start(bf16[128,1024]{1,0:T(8,128)(2,1)S(1)} %get-tuple-element.40), channel_id=1, source_target_pairs={{0,160},{1,161},{2,162},{3,163},{4,164},{5,165},{6,166},{7,167},{8... | collective-permute-start | bytes 786440 | tf_op jit(solution)/shard_map/ppermute | solution.py:26
  143.4 8.6 %collective-permute-start.34 = (bf16[2,2,16,1024]{3,2,1,0:T(8,128)(2,1)S(1)}, bf16[2,2,16,1024]{3,2,1,0:T(8,128)(2,1)S(1)}, u32[]{:S(2)}, u32[]{:S(2)}) collective-permute-start(bf16[2,2,16,1024]{3,2,1,0:T(8,128)(2,1)S(1)} %pad_maximum_fusion.4), channel_id=1, source_target_pairs={{0,4},{1,5},{2,6},{3,7},{4,8},{5,9},{6,10},{7,11},{8,12},{9,13},{1... | collective-permute-start | bytes 393224 | tf_op jit(solution)/shard_map/ppermute | solution.py:26
  152.0 8.8 %collective-permute-start.37 = (bf16[2,16,1024]{2,1,0:T(8,128)(2,1)S(1)}, bf16[2,16,1024]{2,1,0:T(8,128)(2,1)S(1)}, u32[]{:S(2)}, u32[]{:S(2)}) collective-permute-start(bf16[2,16,1024]{2,1,0:T(8,128)(2,1)S(1)} %fusion.17), channel_id=1, source_target_pairs={{0,16},{1,17},{2,18},{3,19},{4,20},{5,21},{6,22},{7,23},{8,24},{9,... | collective-permute-start | bytes 196616 | tf_op jit(solution)/shard_map/ppermute | solution.py:26
  (9 other events, 112.1 us)

commit v2 on v1

--- a/solution.py
+++ b/solution.py
@@ -52,7 +52,7 @@
     return dot(left, right, (1, 1))
 
 
-SMALL = pl.CostEstimate(flops=1 << 20, bytes_accessed=1 << 20, transcendentals=0)
+SMALL = pl.CostEstimate(flops=1 << 20, bytes_accessed=1 << 23, transcendentals=0)
 
 
 def call(kernel, grid, in_specs, out_specs, out_shape, limit, scratch=()):

time: 162 us -> 162 us (level)
  no operation moved by 1% of the time
where the time goes in v2:
time: 162 us
  waiting for transfers between devices  78.5 us (48%)
  starting transfers between devices  55.6 us (34%)
  Pallas kernels  22.7 us (14%)
  other arithmetic  3.02 us (2%)
    ppermute x38, waiting for transfers between devices, send(): lax.ppermute(array, AXES, permutation(lambda a, b, c, d, e: (a ^ x, b ^ y...  78.5 us
    ppermute x38, starting transfers between devices, send(): lax.ppermute(array, AXES, permutation(lambda a, b, c, d, e: (a ^ x, b ^ y...  55.6 us
    pallas_call x2, Pallas kernels, weight_grad(): call(weight_grad_kernel, 2, [side, side] + [whole(g.shape) for g in grads...  7.26 us
    pallas_call x1, Pallas kernels, token_grads(): call(token_grad_kernel, 2, [whole(gates.shape), whole(gates.shape), whole...  6.62 us
    pallas_call x1, Pallas kernels, up_blocks(): call(up_kernel, 2, [half, half, whole(shape), whole(shape)], [pl.BlockSpe...  3.84 us
  transfers between devices with their start and end apart: 38, of which 20 were waited for; matrix products, arithmetic and copies ran while one was open for 1% of the time, Pallas kernels for 14%

profile of v2, /device:TPU:2, one launch (start us, length us, event | category | flops | bytes accessed | tf_op | source)
XLA Modules:
  0.0 161.6 jit_solution(16288758792894431861)
XLA Ops:
  2.0 3.3 %collective-permute-start = (bf16[16,1024]{1,0:T(8,128)(2,1)S(1)}, bf16[16,1024]{1,0:T(8,128)(2,1)S(1)}, u32[]{:S(2)}, u32[]{:S(2)}) collective-permute-start(bf16[16,1024]{1,0:T(8,128)(2,1)S(1)} %pad_maximum_fusion.8), channel_id=1, source_target_pairs={{0,128},{1,129},{2,130},{3,131},{4,132},{5,133},{6,134},{7,135},{8... | collective-permute-start | bytes 98312 | tf_op jit(solution)/shard_map/ppermute | solution.py:26
  5.3 7.2 %collective-permute-start.1 = (bf16[16,1024]{1,0:T(8,128)(2,1)S(1)}, bf16[16,1024]{1,0:T(8,128)(2,1)S(1)}, u32[]{:S(2)}, u32[]{:S(2)}) collective-permute-start(bf16[16,1024]{1,0:T(8,128)(2,1)S(1)} %pad_maximum_fusion.7.refs_0_), channel_id=1, source_target_pairs={{0,16},{1,17},{2,18},{3,19},{4,20},{5,21},{6,22},{7,23},{8,24},{9,... | collective-permute-start | bytes 98312 | tf_op jit(solution)/shard_map/ppermute | solution.py:26
  12.5 1.9 %collective-permute-done.1.refs_2_ = bf16[16,1024]{1,0:T(8,128)(2,1)S(1)} collective-permute-done((bf16[16,1024]{1,0:T(8,128)(2,1)S(1)}, bf16[16,1024]{1,0:T(8,128)(2,1)S(1)}, u32[]{:S(2)}, u32[]{:S(2)}) %collective-permute-start.1) | collective-permute-done | bytes 32800 | tf_op jit(solution)/shard_map/ppermute | solution.py:26
  14.4 8.3 %collective-permute-done.2.refs_3_ = bf16[16,1024]{1,0:T(8,128)(2,1)S(1)} collective-permute-done((bf16[16,1024]{1,0:T(8,128)(2,1)S(1)}, bf16[16,1024]{1,0:T(8,128)(2,1)S(1)}, u32[]{:S(2)}, u32[]{:S(2)}) %collective-permute-start.2) | collective-permute-done | bytes 32800 | tf_op jit(solution)/shard_map/ppermute | solution.py:26
  25.3 2.2 %collective-permute-start.4 = (bf16[64,1024]{1,0:T(8,128)(2,1)S(1)}, bf16[64,1024]{1,0:T(8,128)(2,1)S(1)}, u32[]{:S(2)}, u32[]{:S(2)}) collective-permute-start(bf16[64,1024]{1,0:T(8,128)(2,1)S(1)} %get-tuple-element.25.refs_0_), channel_id=1, source_target_pairs={{0,28},{1,29},{2,30},{3,31},{4,0},{5,1},{6,2},{7,3},{8,4},{9,5},{1... | collective-permute-start | bytes 393224 | tf_op jit(solution)/shard_map/ppermute | solution.py:26
  27.5 2.0 %collective-permute-done.5.refs_3_ = bf16[32,1024]{1,0:T(8,128)(2,1)S(1)} collective-permute-done((bf16[32,1024]{1,0:T(8,128)(2,1)S(1)}, bf16[32,1024]{1,0:T(8,128)(2,1)S(1)}, u32[]{:S(2)}, u32[]{:S(2)}) %collective-permute-start.5) | collective-permute-done | bytes 65568 | tf_op jit(solution)/shard_map/ppermute | solution.py:26
  29.6 5.2 %collective-permute-done.6.refs_4_ = bf16[32,1024]{1,0:T(8,128)(2,1)S(1)} collective-permute-done((bf16[32,1024]{1,0:T(8,128)(2,1)S(1)}, bf16[32,1024]{1,0:T(8,128)(2,1)S(1)}, u32[]{:S(2)}, u32[]{:S(2)}) %collective-permute-start.6) | collective-permute-done | bytes 65568 | tf_op jit(solution)/shard_map/ppermute | solution.py:26
  36.5 9.4 %collective-permute-done.7.second = bf16[256,1024]{1,0:T(8,128)(2,1)} collective-permute-done((bf16[256,1024]{1,0:T(8,128)(2,1)}, bf16[256,1024]{1,0:T(8,128)(2,1)}, u32[]{:S(2)}, u32[]{:S(2)}) %collective-permute-start.7) | collective-permute-done | bytes 524320 | tf_op jit(solution)/shard_map/ppermute | solution.py:26
  45.8 1.9 %shard_map.77 = (bf16[512,512]{1,0:T(8,128)(2,1)S(1)}, bf16[512,512]{1,0:T(8,128)(2,1)S(1)}) custom-call(bf16[256,1024]{1,0:T(8,128)(2,1)} %shard_map.76.first, bf16[256,1024]{1,0:T(8,128)(2,1)} %collective-permute-done.7.second, bf16[512,512]{1,0:T(8,128)(2,1)S(1)} %fusion.order), custom_call_target="tpu_custom_call" | custom-call | flops 1048576 | bytes 8388608 | tf_op jit(solution)/shard_map/pallas_call | solution.py:180
  47.8 3.8 %shard_map.80 = (bf16[2,64,1664]{2,1,0:T(8,128)(2,1)S(1)}, bf16[2,64,1664]{2,1,0:T(8,128)(2,1)S(1)}, bf16[2,64,1664]{2,1,0:T(8,128)(2,1)S(1)}, bf16[2,64,1664]{2,1,0:T(8,128)(2,1)S(1)}) custom-call(bf16[512,512]{1,0:T(8,128)(2,1)S(1)} %get-tuple-element.27.near.refs_0_, bf16[512,512]{1,0:T(8,128)(2,1)S(1)} %get-tuple-element.28.distant, ...), custom_call_target="tpu_custom_call" | custom-call | flops 1048576 | bytes 8388608 | tf_op jit(solution)/shard_map/pallas_call | solution.py:135
  58.3 9.5 %collective-permute-done.16 = bf16[2,64,1664]{2,1,0:T(8,128)(2,1)S(1)} collective-permute-done((bf16[2,64,1664]{2,1,0:T(8,128)(2,1)S(1)}, bf16[2,64,1664]{2,1,0:T(8,128)(2,1)S(1)}, u32[]{:S(2)}, u32[]{:S(2)}) %collective-permute-start.16) | collective-permute-done | bytes 426016 | tf_op jit(solution)/shard_map/ppermute | solution.py:26
  69.9 2.2 %collective-permute-start.17 = (bf16[64,1664]{1,0:T(8,128)(2,1)S(1)}, bf16[64,1664]{1,0:T(8,128)(2,1)S(1)}, u32[]{:S(2)}, u32[]{:S(2)}) collective-permute-start(bf16[64,1664]{1,0:T(8,128)(2,1)S(1)} %slice_bitcast_fusion), channel_id=1, source_target_pairs={{0,128},{1,129},{2,130},{3,131},{4,132},{5,133},{6,134},{7,135},{8... | collective-permute-start | bytes 638984 | tf_op jit(solution)/shard_map/ppermute | solution.py:26
  72.1 4.0 %collective-permute-done.9.far = bf16[256,1664]{1,0:T(8,128)(2,1)S(1)} collective-permute-done((bf16[256,1664]{1,0:T(8,128)(2,1)S(1)}, bf16[256,1664]{1,0:T(8,128)(2,1)S(1)}, u32[]{:S(2)}, u32[]{:S(2)}) %collective-permute-start.9) | collective-permute-done | bytes 852000 | tf_op jit(solution)/shard_map/ppermute | solution.py:26
  83.1 3.1 %collective-permute-done.11 = bf16[64,1664]{1,0:T(8,128)(2,1)S(1)} collective-permute-done((bf16[64,1664]{1,0:T(8,128)(2,1)S(1)}, bf16[64,1664]{1,0:T(8,128)(2,1)S(1)}, u32[]{:S(2)}, u32[]{:S(2)}) %collective-permute-start.11) | collective-permute-done | bytes 213024 | tf_op jit(solution)/shard_map/ppermute | solution.py:26
  86.2 2.5 %collective-permute-done.10 = bf16[64,1664]{1,0:T(8,128)(2,1)S(1)} collective-permute-done((bf16[64,1664]{1,0:T(8,128)(2,1)S(1)}, bf16[64,1664]{1,0:T(8,128)(2,1)S(1)}, u32[]{:S(2)}, u32[]{:S(2)}) %collective-permute-start.10) | collective-permute-done | bytes 213024 | tf_op jit(solution)/shard_map/ppermute | solution.py:26
  91.0 1.9 %collective-permute-start.20 = (bf16[64,1664]{1,0:T(8,128)(2,1)S(1)}, bf16[64,1664]{1,0:T(8,128)(2,1)S(1)}, u32[]{:S(2)}, u32[]{:S(2)}) collective-permute-start(bf16[64,1664]{1,0:T(8,128)(2,1)S(1)} %get-tuple-element.46), channel_id=1, source_target_pairs={{0,3},{1,2},{2,1},{3,0},{4,7},{5,6},{6,5},{7,4},{8,11},{9,10},{10,... | collective-permute-start | bytes 638984 | tf_op jit(solution)/shard_map/ppermute | solution.py:26
  92.9 2.2 %collective-permute-start.18 = (bf16[64,1664]{1,0:T(8,128)(2,1)S(1)}, bf16[64,1664]{1,0:T(8,128)(2,1)S(1)}, u32[]{:S(2)}, u32[]{:S(2)}) collective-permute-start(bf16[64,1664]{1,0:T(8,128)(2,1)S(1)} %get-tuple-element.46), channel_id=1, source_target_pairs={{0,1},{1,0},{2,3},{3,2},{4,5},{5,4},{6,7},{7,6},{8,9},{9,8},{10,11... | collective-permute-start | bytes 638984 | tf_op jit(solution)/shard_map/ppermute | solution.py:26
  95.1 2.8 %collective-permute-done.22 = bf16[64,1664]{1,0:T(8,128)(2,1)S(1)} collective-permute-done((bf16[64,1664]{1,0:T(8,128)(2,1)S(1)}, bf16[64,1664]{1,0:T(8,128)(2,1)S(1)}, u32[]{:S(2)}, u32[]{:S(2)}) %collective-permute-start.22) | collective-permute-done | bytes 213024 | tf_op jit(solution)/shard_map/ppermute | solution.py:26
  98.0 2.5 %collective-permute-start.25 = (bf16[2,64,1664]{2,1,0:T(8,128)(2,1)S(1)}, bf16[2,64,1664]{2,1,0:T(8,128)(2,1)S(1)}, u32[]{:S(2)}, u32[]{:S(2)}) collective-permute-start(bf16[2,64,1664]{2,1,0:T(8,128)(2,1)S(1)} %get-tuple-element.56), channel_id=1, source_target_pairs={{0,3},{1,2},{2,1},{3,0},{4,7},{5,6},{6,5},{7,4},{8,11},{9,10},{10,... | collective-permute-start | bytes 1277960 | tf_op jit(solution)/shard_map/ppermute | solution.py:26
  100.5 3.8 %collective-permute-done.20 = bf16[64,1664]{1,0:T(8,128)(2,1)S(1)} collective-permute-done((bf16[64,1664]{1,0:T(8,128)(2,1)S(1)}, bf16[64,1664]{1,0:T(8,128)(2,1)S(1)}, u32[]{:S(2)}, u32[]{:S(2)}) %collective-permute-start.20) | collective-permute-done | bytes 213024 | tf_op jit(solution)/shard_map/ppermute | solution.py:26
  106.1 2.1 %collective-permute-start.21 = (bf16[256,1664]{1,0:T(8,128)(2,1)S(1)}, bf16[256,1664]{1,0:T(8,128)(2,1)S(1)}, u32[]{:S(2)}, u32[]{:S(2)}) collective-permute-start(bf16[256,1664]{1,0:T(8,128)(2,1)S(1)} %pad_maximum_fusion.1.gates.refs_2_), channel_id=1, source_target_pairs={{0,128},{1,129},{2,130},{3,131},{4,132},{5,133},{6,134},{7,135},{8... | collective-permute-start | bytes 2555912 | tf_op jit(solution)/shard_map/ppermute | solution.py:26
  108.2 5.3 %collective-permute-done.25 = bf16[2,64,1664]{2,1,0:T(8,128)(2,1)S(1)} collective-permute-done((bf16[2,64,1664]{2,1,0:T(8,128)(2,1)S(1)}, bf16[2,64,1664]{2,1,0:T(8,128)(2,1)S(1)}, u32[]{:S(2)}, u32[]{:S(2)}) %collective-permute-start.25) | collective-permute-done | bytes 426016 | tf_op jit(solution)/shard_map/ppermute | solution.py:26
  116.0 4.4 %collective-permute-done.21.far_gates.refs_3_ = bf16[256,1664]{1,0:T(8,128)(2,1)S(1)} collective-permute-done((bf16[256,1664]{1,0:T(8,128)(2,1)S(1)}, bf16[256,1664]{1,0:T(8,128)(2,1)S(1)}, u32[]{:S(2)}, u32[]{:S(2)}) %collective-permute-start.21) | collective-permute-done | bytes 852000 | tf_op jit(solution)/shard_map/ppermute | solution.py:26
  121.1 6.6 %shard_map.81 = (bf16[128,1024]{1,0:T(8,128)(2,1)S(1)}, bf16[128,1024]{1,0:T(8,128)(2,1)S(1)}, bf16[128,1024]{1,0:T(8,128)(2,1)S(1)}, bf16[128,1024]{1,0:T(8,128)(2,1)S(1)}) custom-call(bf16[256,1664]{1,0:T(8,128)(2,1)S(1)} %pad_maximum_fusion.1.gates.refs_2_, bf16[256,1664]{1,0:T(8,128)(2,1)S(1)} %collective-permute-done.21.far_gates.refs_3_, ...), custom_call_target="tpu_custom_call" | custom-call | flops 1048576 | bytes 8388608 | tf_op jit(solution)/shard_map/pallas_call | solution.py:219
  127.7 2.1 %collective-permute-start.26 = (bf16[128,1024]{1,0:T(8,128)(2,1)S(1)}, bf16[128,1024]{1,0:T(8,128)(2,1)S(1)}, u32[]{:S(2)}, u32[]{:S(2)}) collective-permute-start(bf16[128,1024]{1,0:T(8,128)(2,1)S(1)} %get-tuple-element.38), channel_id=1, source_target_pairs={{0,128},{1,129},{2,130},{3,131},{4,132},{5,133},{6,134},{7,135},{8... | collective-permute-start | bytes 786440 | tf_op jit(solution)/shard_map/ppermute | solution.py:26
  129.8 2.1 %collective-permute-start.28 = (bf16[128,1024]{1,0:T(8,128)(2,1)S(1)}, bf16[128,1024]{1,0:T(8,128)(2,1)S(1)}, u32[]{:S(2)}, u32[]{:S(2)}) collective-permute-start(bf16[128,1024]{1,0:T(8,128)(2,1)S(1)} %get-tuple-element.40), channel_id=1, source_target_pairs={{0,160},{1,161},{2,162},{3,163},{4,164},{5,165},{6,166},{7,167},{8... | collective-permute-start | bytes 786440 | tf_op jit(solution)/shard_map/ppermute | solution.py:26
  131.9 3.6 %shard_map.82 = f32[512,1664]{1,0:T(8,128)} custom-call(bf16[512,512]{1,0:T(8,128)(2,1)S(1)} %get-tuple-element.27.near.refs_0_, bf16[512,512]{1,0:T(8,128)(2,1)S(1)} %collective-permute-done.29.refs_1_, bf16[256,1664]{1,0:T(8,128)(2,1)S(1)} %pad_maximum_fusion.1.gates.refs_2_, bf16[256,1664]{1,0:T(8,128)(2,1)S(1)} %collective-permute-done.21.far_gates.refs_3_, ...), custom_call_target="tpu_custom_call" | custom-call | flops 1048576 | bytes 8388608 | tf_op jit(solution)/shard_map/pallas_call | solution.py:248
  135.5 3.6 %shard_map.83 = f32[512,1664]{1,0:T(8,128)} custom-call(bf16[512,512]{1,0:T(8,128)(2,1)S(1)} %get-tuple-element.27.near.refs_0_, bf16[512,512]{1,0:T(8,128)(2,1)S(1)} %collective-permute-done.29.refs_1_, bf16[512,1664]{1,0:T(8,128)(2,1)S(1)} %bitcast.43, bf16[512,1664]{1,0:T(8,128)(2,1)S(1)} %collective-permute-done.32.refs_3_), custom_call_target="tpu_custom_call" | custom-call | flops 1048576 | bytes 8388608 | tf_op jit(solution)/shard_map/pallas_call | solution.py:248
  139.1 2.3 %collective-permute-done.27 = bf16[128,1024]{1,0:T(8,128)(2,1)S(1)} collective-permute-done((bf16[128,1024]{1,0:T(8,128)(2,1)S(1)}, bf16[128,1024]{1,0:T(8,128)(2,1)S(1)}, u32[]{:S(2)}, u32[]{:S(2)}) %collective-permute-start.27) | collective-permute-done | bytes 262176 | tf_op jit(solution)/shard_map/ppermute | solution.py:26
  144.7 3.1 %collective-permute-start.33 = (bf16[2,2,16,1024]{3,2,1,0:T(8,128)(2,1)S(1)}, bf16[2,2,16,1024]{3,2,1,0:T(8,128)(2,1)S(1)}, u32[]{:S(2)}, u32[]{:S(2)}) collective-permute-start(bf16[2,2,16,1024]{3,2,1,0:T(8,128)(2,1)S(1)} %pad_maximum_fusion.3), channel_id=1, source_target_pairs={{0,28},{1,29},{2,30},{3,31},{4,0},{5,1},{6,2},{7,3},{8,4},{9,5},{1... | collective-permute-start | bytes 393224 | tf_op jit(solution)/shard_map/ppermute | solution.py:26
  147.8 4.1 %collective-permute-start.35 = (bf16[2,16,1024]{2,1,0:T(8,128)(2,1)S(1)}, bf16[2,16,1024]{2,1,0:T(8,128)(2,1)S(1)}, u32[]{:S(2)}, u32[]{:S(2)}) collective-permute-start(bf16[2,16,1024]{2,1,0:T(8,128)(2,1)S(1)} %get-tuple-element.49), channel_id=1, source_target_pairs={{0,24},{1,25},{2,26},{3,27},{4,28},{5,29},{6,30},{7,31},{8,0},{9,1... | collective-permute-start | bytes 196616 | tf_op jit(solution)/shard_map/ppermute | solution.py:26
  155.0 5.9 %collective-permute-done.37 = bf16[2,16,1024]{2,1,0:T(8,128)(2,1)S(1)} collective-permute-done((bf16[2,16,1024]{2,1,0:T(8,128)(2,1)S(1)}, bf16[2,16,1024]{2,1,0:T(8,128)(2,1)S(1)}, u32[]{:S(2)}, u32[]{:S(2)}) %collective-permute-start.37) | collective-permute-done | bytes 65568 | tf_op jit(solution)/shard_map/ppermute | solution.py:26
  (83 shorter events, 35.9 us)
Async XLA Ops:
  0.6 47.1 %collective-permute-start.13 = (bf16[512,1664]{1,0:T(8,128)(2,1)}, bf16[512,1664]{1,0:T(8,128)(2,1)}, u32[]{:S(2)}, u32[]{:S(2)}) collective-permute-start(bf16[512,1664]{1,0:T(8,128)(2,1)} %wu0.1), channel_id=1, source_target_pairs={{0,64},{1,65},{2,66},{3,67},{4,68},{5,69},{6,70},{7,71},{8,72},{9,... | collective-permute-start | bytes 5111816 | tf_op jit(solution)/shard_map/ppermute | solution.py:26
  0.7 55.1 %collective-permute-start.8 = (bf16[512,1664]{1,0:T(8,128)(2,1)}, bf16[512,1664]{1,0:T(8,128)(2,1)S(1)}, u32[]{:S(2)}, u32[]{:S(2)}) collective-permute-start(bf16[512,1664]{1,0:T(8,128)(2,1)} %wg0.1), channel_id=1, source_target_pairs={{0,64},{1,65},{2,66},{3,67},{4,68},{5,69},{6,70},{7,71},{8,72},{9,... | collective-permute-start | bytes 5111816 | tf_op jit(solution)/shard_map/ppermute | solution.py:26
  2.0 10.5 %collective-permute-start = (bf16[16,1024]{1,0:T(8,128)(2,1)S(1)}, bf16[16,1024]{1,0:T(8,128)(2,1)S(1)}, u32[]{:S(2)}, u32[]{:S(2)}) collective-permute-start(bf16[16,1024]{1,0:T(8,128)(2,1)S(1)} %pad_maximum_fusion.8), channel_id=1, source_target_pairs={{0,128},{1,129},{2,130},{3,131},{4,132},{5,133},{6,134},{7,135},{8... | collective-permute-start | bytes 98312 | tf_op jit(solution)/shard_map/ppermute | solution.py:26
  5.3 9.1 %collective-permute-start.1 = (bf16[16,1024]{1,0:T(8,128)(2,1)S(1)}, bf16[16,1024]{1,0:T(8,128)(2,1)S(1)}, u32[]{:S(2)}, u32[]{:S(2)}) collective-permute-start(bf16[16,1024]{1,0:T(8,128)(2,1)S(1)} %pad_maximum_fusion.7.refs_0_), channel_id=1, source_target_pairs={{0,16},{1,17},{2,18},{3,19},{4,20},{5,21},{6,22},{7,23},{8,24},{9,... | collective-permute-start | bytes 98312 | tf_op jit(solution)/shard_map/ppermute | solution.py:26
  12.5 10.2 %collective-permute-start.2 = (bf16[16,1024]{1,0:T(8,128)(2,1)S(1)}, bf16[16,1024]{1,0:T(8,128)(2,1)S(1)}, u32[]{:S(2)}, u32[]{:S(2)}) collective-permute-start(bf16[16,1024]{1,0:T(8,128)(2,1)S(1)} %pad_maximum_fusion.8), channel_id=1, source_target_pairs={{0,144},{1,145},{2,146},{3,147},{4,148},{5,149},{6,150},{7,151},{8... | collective-permute-start | bytes 98312 | tf_op jit(solution)/shard_map/ppermute | solution.py:26
  24.3 10.4 %collective-permute-start.3 = (bf16[64,1024]{1,0:T(8,128)(2,1)S(1)}, bf16[64,1024]{1,0:T(8,128)(2,1)S(1)}, u32[]{:S(2)}, u32[]{:S(2)}) collective-permute-start(bf16[64,1024]{1,0:T(8,128)(2,1)S(1)} %get-tuple-element.25.refs_0_), channel_id=1, source_target_pairs={{0,4},{1,5},{2,6},{3,7},{4,8},{5,9},{6,10},{7,11},{8,12},{9,13},{1... | collective-permute-start | bytes 393224 | tf_op jit(solution)/shard_map/ppermute | solution.py:26
  25.3 9.4 %collective-permute-start.4 = (bf16[64,1024]{1,0:T(8,128)(2,1)S(1)}, bf16[64,1024]{1,0:T(8,128)(2,1)S(1)}, u32[]{:S(2)}, u32[]{:S(2)}) collective-permute-start(bf16[64,1024]{1,0:T(8,128)(2,1)S(1)} %get-tuple-element.25.refs_0_), channel_id=1, source_target_pairs={{0,28},{1,29},{2,30},{3,31},{4,0},{5,1},{6,2},{7,3},{8,4},{9,5},{1... | collective-permute-start | bytes 393224 | tf_op jit(solution)/shard_map/ppermute | solution.py:26
  35.6 10.3 %collective-permute-start.7 = (bf16[256,1024]{1,0:T(8,128)(2,1)}, bf16[256,1024]{1,0:T(8,128)(2,1)}, u32[]{:S(2)}, u32[]{:S(2)}) collective-permute-start(bf16[256,1024]{1,0:T(8,128)(2,1)} %shard_map.76.first), channel_id=1, source_target_pairs={{0,32},{1,33},{2,34},{3,35},{4,36},{5,37},{6,38},{7,39},{8,40},{9,... | collective-permute-start | bytes 1572872 | tf_op jit(solution)/shard_map/ppermute | solution.py:26
  51.6 16.1 %collective-permute-start.16 = (bf16[2,64,1664]{2,1,0:T(8,128)(2,1)S(1)}, bf16[2,64,1664]{2,1,0:T(8,128)(2,1)S(1)}, u32[]{:S(2)}, u32[]{:S(2)}) collective-permute-start(bf16[2,64,1664]{2,1,0:T(8,128)(2,1)S(1)} %get-tuple-element.36), channel_id=1, source_target_pairs={{0,3},{1,2},{2,1},{3,0},{4,7},{5,6},{6,5},{7,4},{8,11},{9,10},{10,... | collective-permute-start | bytes 1277960 | tf_op jit(solution)/shard_map/ppermute | solution.py:26
  53.2 14.6 %collective-permute-start.15 = (bf16[2,64,1664]{2,1,0:T(8,128)(2,1)S(1)}, bf16[2,64,1664]{2,1,0:T(8,128)(2,1)S(1)}, u32[]{:S(2)}, u32[]{:S(2)}) collective-permute-start(bf16[2,64,1664]{2,1,0:T(8,128)(2,1)S(1)} %get-tuple-element.35), channel_id=1, source_target_pairs={{0,2},{1,3},{2,0},{3,1},{4,6},{5,7},{6,4},{7,5},{8,10},{9,11},{10,... | collective-permute-start | bytes 1277960 | tf_op jit(solution)/shard_map/ppermute | solution.py:26
  54.3 15.3 %collective-permute-start.14 = (bf16[2,64,1664]{2,1,0:T(8,128)(2,1)S(1)}, bf16[2,64,1664]{2,1,0:T(8,128)(2,1)S(1)}, u32[]{:S(2)}, u32[]{:S(2)}) collective-permute-start(bf16[2,64,1664]{2,1,0:T(8,128)(2,1)S(1)} %get-tuple-element.34), channel_id=1, source_target_pairs={{0,1},{1,0},{2,3},{3,2},{4,5},{5,4},{6,7},{7,6},{8,9},{9,8},{10,11... | collective-permute-start | bytes 1277960 | tf_op jit(solution)/shard_map/ppermute | solution.py:26
  56.9 19.1 %collective-permute-start.9 = (bf16[256,1664]{1,0:T(8,128)(2,1)S(1)}, bf16[256,1664]{1,0:T(8,128)(2,1)S(1)}, u32[]{:S(2)}, u32[]{:S(2)}) collective-permute-start(bf16[256,1664]{1,0:T(8,128)(2,1)S(1)} %shard_map.78), channel_id=1, source_target_pairs={{0,128},{1,129},{2,130},{3,131},{4,132},{5,133},{6,134},{7,135},{8... | collective-permute-start | bytes 2555912 | tf_op jit(solution)/shard_map/ppermute | solution.py:26
  69.9 11.4 %collective-permute-start.17 = (bf16[64,1664]{1,0:T(8,128)(2,1)S(1)}, bf16[64,1664]{1,0:T(8,128)(2,1)S(1)}, u32[]{:S(2)}, u32[]{:S(2)}) collective-permute-start(bf16[64,1664]{1,0:T(8,128)(2,1)S(1)} %slice_bitcast_fusion), channel_id=1, source_target_pairs={{0,128},{1,129},{2,130},{3,131},{4,132},{5,133},{6,134},{7,135},{8... | collective-permute-start | bytes 638984 | tf_op jit(solution)/shard_map/ppermute | solution.py:26
  78.7 7.5 %collective-permute-start.11 = (bf16[64,1664]{1,0:T(8,128)(2,1)S(1)}, bf16[64,1664]{1,0:T(8,128)(2,1)S(1)}, u32[]{:S(2)}, u32[]{:S(2)}) collective-permute-start(bf16[64,1664]{1,0:T(8,128)(2,1)S(1)} %get-tuple-element.31), channel_id=1, source_target_pairs={{0,2},{1,3},{2,0},{3,1},{4,6},{5,7},{6,4},{7,5},{8,10},{9,11},{10,... | collective-permute-start | bytes 638984 | tf_op jit(solution)/shard_map/ppermute | solution.py:26
  79.7 8.9 %collective-permute-start.10 = (bf16[64,1664]{1,0:T(8,128)(2,1)S(1)}, bf16[64,1664]{1,0:T(8,128)(2,1)S(1)}, u32[]{:S(2)}, u32[]{:S(2)}) collective-permute-start(bf16[64,1664]{1,0:T(8,128)(2,1)S(1)} %get-tuple-element.30), channel_id=1, source_target_pairs={{0,1},{1,0},{2,3},{3,2},{4,5},{5,4},{6,7},{7,6},{8,9},{9,8},{10,11... | collective-permute-start | bytes 638984 | tf_op jit(solution)/shard_map/ppermute | solution.py:26
  89.7 8.2 %collective-permute-start.22 = (bf16[64,1664]{1,0:T(8,128)(2,1)S(1)}, bf16[64,1664]{1,0:T(8,128)(2,1)S(1)}, u32[]{:S(2)}, u32[]{:S(2)}) collective-permute-start(bf16[64,1664]{1,0:T(8,128)(2,1)S(1)} %get-tuple-element.48), channel_id=1, source_target_pairs={{0,128},{1,129},{2,130},{3,131},{4,132},{5,133},{6,134},{7,135},{8... | collective-permute-start | bytes 638984 | tf_op jit(solution)/shard_map/ppermute | solution.py:26
  91.0 13.3 %collective-permute-start.20 = (bf16[64,1664]{1,0:T(8,128)(2,1)S(1)}, bf16[64,1664]{1,0:T(8,128)(2,1)S(1)}, u32[]{:S(2)}, u32[]{:S(2)}) collective-permute-start(bf16[64,1664]{1,0:T(8,128)(2,1)S(1)} %get-tuple-element.46), channel_id=1, source_target_pairs={{0,3},{1,2},{2,1},{3,0},{4,7},{5,6},{6,5},{7,4},{8,11},{9,10},{10,... | collective-permute-start | bytes 638984 | tf_op jit(solution)/shard_map/ppermute | solution.py:26
  92.9 13.1 %collective-permute-start.19 = (bf16[64,1664]{1,0:T(8,128)(2,1)S(1)}, bf16[64,1664]{1,0:T(8,128)(2,1)S(1)}, u32[]{:S(2)}, u32[]{:S(2)}) collective-permute-start(bf16[64,1664]{1,0:T(8,128)(2,1)S(1)} %get-tuple-element.46), channel_id=1, source_target_pairs={{0,2},{1,3},{2,0},{3,1},{4,6},{5,7},{6,4},{7,5},{8,10},{9,11},{10,... | collective-permute-start | bytes 638984 | tf_op jit(solution)/shard_map/ppermute | solution.py:26
  92.9 13.1 %collective-permute-start.18 = (bf16[64,1664]{1,0:T(8,128)(2,1)S(1)}, bf16[64,1664]{1,0:T(8,128)(2,1)S(1)}, u32[]{:S(2)}, u32[]{:S(2)}) collective-permute-start(bf16[64,1664]{1,0:T(8,128)(2,1)S(1)} %get-tuple-element.46), channel_id=1, source_target_pairs={{0,1},{1,0},{2,3},{3,2},{4,5},{5,4},{6,7},{7,6},{8,9},{9,8},{10,11... | collective-permute-start | bytes 638984 | tf_op jit(solution)/shard_map/ppermute | solution.py:26
  98.0 15.5 %collective-permute-start.25 = (bf16[2,64,1664]{2,1,0:T(8,128)(2,1)S(1)}, bf16[2,64,1664]{2,1,0:T(8,128)(2,1)S(1)}, u32[]{:S(2)}, u32[]{:S(2)}) collective-permute-start(bf16[2,64,1664]{2,1,0:T(8,128)(2,1)S(1)} %get-tuple-element.56), channel_id=1, source_target_pairs={{0,3},{1,2},{2,1},{3,0},{4,7},{5,6},{6,5},{7,4},{8,11},{9,10},{10,... | collective-permute-start | bytes 1277960 | tf_op jit(solution)/shard_map/ppermute | solution.py:26
  100.5 12.9 %collective-permute-start.24 = (bf16[2,64,1664]{2,1,0:T(8,128)(2,1)S(1)}, bf16[2,64,1664]{2,1,0:T(8,128)(2,1)S(1)}, u32[]{:S(2)}, u32[]{:S(2)}) collective-permute-start(bf16[2,64,1664]{2,1,0:T(8,128)(2,1)S(1)} %get-tuple-element.56), channel_id=1, source_target_pairs={{0,2},{1,3},{2,0},{3,1},{4,6},{5,7},{6,4},{7,5},{8,10},{9,11},{10,... | collective-permute-start | bytes 1277960 | tf_op jit(solution)/shard_map/ppermute | solution.py:26
  104.3 10.6 %collective-permute-start.23 = (bf16[2,64,1664]{2,1,0:T(8,128)(2,1)S(1)}, bf16[2,64,1664]{2,1,0:T(8,128)(2,1)S(1)}, u32[]{:S(2)}, u32[]{:S(2)}) collective-permute-start(bf16[2,64,1664]{2,1,0:T(8,128)(2,1)S(1)} %get-tuple-element.56), channel_id=1, source_target_pairs={{0,1},{1,0},{2,3},{3,2},{4,5},{5,4},{6,7},{7,6},{8,9},{9,8},{10,11... | collective-permute-start | bytes 1277960 | tf_op jit(solution)/shard_map/ppermute | solution.py:26
  106.1 14.3 %collective-permute-start.21 = (bf16[256,1664]{1,0:T(8,128)(2,1)S(1)}, bf16[256,1664]{1,0:T(8,128)(2,1)S(1)}, u32[]{:S(2)}, u32[]{:S(2)}) collective-permute-start(bf16[256,1664]{1,0:T(8,128)(2,1)S(1)} %pad_maximum_fusion.1.gates.refs_2_), channel_id=1, source_target_pairs={{0,128},{1,129},{2,130},{3,131},{4,132},{5,133},{6,134},{7,135},{8... | collective-permute-start | bytes 2555912 | tf_op jit(solution)/shard_map/ppermute | solution.py:26
  115.4 20.1 %collective-permute-start.32 = (bf16[512,1664]{1,0:T(8,128)(2,1)S(1)}, bf16[512,1664]{1,0:T(8,128)(2,1)S(1)}, u32[]{:S(2)}, u32[]{:S(2)}) collective-permute-start(bf16[512,1664]{1,0:T(8,128)(2,1)S(1)} %bitcast.41), channel_id=1, source_target_pairs={{0,64},{1,65},{2,66},{3,67},{4,68},{5,69},{6,70},{7,71},{8,72},{9,... | collective-permute-start | bytes 5111816 | tf_op jit(solution)/shard_map/ppermute | solution.py:26
  115.5 14.3 %collective-permute-start.30 = (bf16[256,1664]{1,0:T(8,128)(2,1)S(1)}, bf16[256,1664]{1,0:T(8,128)(2,1)S(1)}, u32[]{:S(2)}, u32[]{:S(2)}) collective-permute-start(bf16[256,1664]{1,0:T(8,128)(2,1)S(1)} %pad_maximum_fusion.1.gates.refs_2_), channel_id=1, source_target_pairs={{0,64},{1,65},{2,66},{3,67},{4,68},{5,69},{6,70},{7,71},{8,72},{9,... | collective-permute-start | bytes 2555912 | tf_op jit(solution)/shard_map/ppermute | solution.py:26
  120.4 11.5 %collective-permute-start.31 = (bf16[256,1664]{1,0:T(8,128)(2,1)S(1)}, bf16[256,1664]{1,0:T(8,128)(2,1)S(1)}, u32[]{:S(2)}, u32[]{:S(2)}) collective-permute-start(bf16[256,1664]{1,0:T(8,128)(2,1)S(1)} %collective-permute-done.21.far_gates.refs_3_), channel_id=1, source_target_pairs={{0,64},{1,65},{2,66},{3,67},{4,68},{5,69},{6,70},{7,71},{8,72},{9,... | collective-permute-start | bytes 2555912 | tf_op jit(solution)/shard_map/ppermute | solution.py:26
  120.4 9.4 %collective-permute-start.29 = (bf16[512,512]{1,0:T(8,128)(2,1)S(1)}, bf16[512,512]{1,0:T(8,128)(2,1)S(1)}, u32[]{:S(2)}, u32[]{:S(2)}) collective-permute-start(bf16[512,512]{1,0:T(8,128)(2,1)S(1)} %get-tuple-element.28.distant), channel_id=1, source_target_pairs={{0,64},{1,65},{2,66},{3,67},{4,68},{5,69},{6,70},{7,71},{8,72},{9,... | collective-permute-start | bytes 1572872 | tf_op jit(solution)/shard_map/ppermute | solution.py:26
  127.7 11.5 %collective-permute-start.26 = (bf16[128,1024]{1,0:T(8,128)(2,1)S(1)}, bf16[128,1024]{1,0:T(8,128)(2,1)S(1)}, u32[]{:S(2)}, u32[]{:S(2)}) collective-permute-start(bf16[128,1024]{1,0:T(8,128)(2,1)S(1)} %get-tuple-element.38), channel_id=1, source_target_pairs={{0,128},{1,129},{2,130},{3,131},{4,132},{5,133},{6,134},{7,135},{8... | collective-permute-start | bytes 786440 | tf_op jit(solution)/shard_map/ppermute | solution.py:26
  129.8 11.7 %collective-permute-start.27 = (bf16[128,1024]{1,0:T(8,128)(2,1)S(1)}, bf16[128,1024]{1,0:T(8,128)(2,1)S(1)}, u32[]{:S(2)}, u32[]{:S(2)}) collective-permute-start(bf16[128,1024]{1,0:T(8,128)(2,1)S(1)} %get-tuple-element.39), channel_id=1, source_target_pairs={{0,32},{1,33},{2,34},{3,35},{4,36},{5,37},{6,38},{7,39},{8,40},{9,... | collective-permute-start | bytes 786440 | tf_op jit(solution)/shard_map/ppermute | solution.py:26
  129.8 13.3 %collective-permute-start.28 = (bf16[128,1024]{1,0:T(8,128)(2,1)S(1)}, bf16[128,1024]{1,0:T(8,128)(2,1)S(1)}, u32[]{:S(2)}, u32[]{:S(2)}) collective-permute-start(bf16[128,1024]{1,0:T(8,128)(2,1)S(1)} %get-tuple-element.40), channel_id=1, source_target_pairs={{0,160},{1,161},{2,162},{3,163},{4,164},{5,165},{6,166},{7,167},{8... | collective-permute-start | bytes 786440 | tf_op jit(solution)/shard_map/ppermute | solution.py:26
  143.4 8.6 %collective-permute-start.34 = (bf16[2,2,16,1024]{3,2,1,0:T(8,128)(2,1)S(1)}, bf16[2,2,16,1024]{3,2,1,0:T(8,128)(2,1)S(1)}, u32[]{:S(2)}, u32[]{:S(2)}) collective-permute-start(bf16[2,2,16,1024]{3,2,1,0:T(8,128)(2,1)S(1)} %pad_maximum_fusion.4), channel_id=1, source_target_pairs={{0,4},{1,5},{2,6},{3,7},{4,8},{5,9},{6,10},{7,11},{8,12},{9,13},{1... | collective-permute-start | bytes 393224 | tf_op jit(solution)/shard_map/ppermute | solution.py:26
  152.0 8.8 %collective-permute-start.37 = (bf16[2,16,1024]{2,1,0:T(8,128)(2,1)S(1)}, bf16[2,16,1024]{2,1,0:T(8,128)(2,1)S(1)}, u32[]{:S(2)}, u32[]{:S(2)}) collective-permute-start(bf16[2,16,1024]{2,1,0:T(8,128)(2,1)S(1)} %fusion.17), channel_id=1, source_target_pairs={{0,16},{1,17},{2,18},{3,19},{4,20},{5,21},{6,22},{7,23},{8,24},{9,... | collective-permute-start | bytes 196616 | tf_op jit(solution)/shard_map/ppermute | solution.py:26
  (9 other events, 112.1 us)
